TPU v7x, 32 devices: a whole 2x2x4 slice. The times are simulated.
32 devices in a mesh: gy: 8 (over z, y), gz: 4 (over x, core).
Axes of the slice: x: 2, y: 2, z: 4, core: 2. Of those that a mesh axis runs over, the one named last changes fastest.
Arguments:
- flow_state: bfloat16 [4, 128, 64, 512], P(None, 'gz', 'gy'), may hold values from -4 to 4
- metric: float32 [3, 3], replicated, may hold values from -0.3 to 1.5, as said below
- deformation_matrix: float32 [3, 3], replicated, may hold values from -0.5 to 0.5
Outputs:
- solenoidal_motion: float32 [3, 128, 64, 512], P(None, 'gz', 'gy')
- heat_content_next: float32 [128, 64, 512], P('gz', 'gy')
Inputs may be any that keep to these rules, and one draw needn't show every extreme that they name: `metric`: diagonal entries lie between 1 and 1.5, off-diagonal entries have magnitude at most 0.3.
All inputs are finite; a program needn't handle non-finite values.
Results may differ from a plain program's by a relative error of at most 0.0003.
Values may be sent and summed in bfloat16 or wider, within the bound.
A program may use at most 128 MiB of HBM per device.

v0:
```python
import numpy as np

import jax
import jax.numpy as jnp
from jax import lax
from jax.sharding import PartitionSpec as P

substep_width = 0.4
high = lax.Precision.HIGH


def halos(block, axis, dim, width):
    count = lax.axis_size(axis)
    forward = [(i, (i + 1) % count) for i in range(count)]
    backward = [((i + 1) % count, i) for i in range(count)]
    low = lax.ppermute(
        lax.slice_in_dim(block, block.shape[dim] - width, None, axis=dim), axis, forward
    )
    high_side = lax.ppermute(lax.slice_in_dim(block, 0, width, axis=dim), axis, backward)
    return jnp.concatenate([low, block, high_side], axis=dim)


def stencil(moved):
    return (
        45.0 * (moved(1) - moved(-1)) - 9.0 * (moved(2) - moved(-2)) + (moved(3) - moved(-3))
    ) / 60.0


def diff_roll(f, along):
    return stencil(lambda offset: jnp.roll(f, -offset, axis=along))


def diff_pad(padded, along):
    extent = padded.shape[along] - 6
    return stencil(lambda o: lax.slice_in_dim(padded, 3 + o, 3 + o + extent, axis=along))


def x_tables(length):
    half = length // 2
    k = np.arange(half)[:, None]
    x = np.arange(length)[None, :]
    angle = 2.0 * np.pi * ((k * x) % length) / length
    c, s = np.cos(angle), -np.sin(angle)
    s[0] = np.where(np.arange(length) % 2 == 0, 1.0, -1.0)
    weight = np.where(np.arange(half) == 0, 1.0, 2.0)[:, None]
    return c, s, weight


def by_owner(re, im, owners):
    half, length = re.shape
    m = half // owners
    return np.concatenate(
        [re.reshape(owners, m, length), im.reshape(owners, m, length)], axis=1
    ).reshape(2 * half, length)


def wave(m, length):
    a = 2.0 * np.pi * m / length
    value = 1.5 * np.sin(a) - 0.3 * np.sin(2 * a) + np.sin(3 * a) / 30.0
    return np.where((2 * m) % length == 0, 0.0, value)


def plane_tables(gy, gz, ey, ez):
    ly, lz = gy * ey, gz * ez
    b = np.repeat(np.arange(ez), ey)
    e = np.tile(np.arange(ey), ez)
    s = np.repeat(np.arange(gy), gz)[:, None]
    q = np.tile(np.arange(gz), gy)[:, None]
    twist = -2.0 * np.pi * (b * q / lz + e * s / ly)
    kron = -2.0 * np.pi * (np.outer(b, b) / ez + np.outer(e, e) / ey)
    my = gy * e[None, :] + s
    mz = gz * b[None, :] + q
    block = -2.0 * np.pi * (
        np.outer(s, s) / gy + np.outer(q, q) / gz
    )
    edge = ((2 * my) % ly == 0) & ((2 * mz) % lz == 0)
    return twist, kron, block, wave(my, ly), wave(mz, lz), edge


def f32(a):
    return jnp.asarray(np.asarray(a, np.float32))


def shards(flow_state, metric, deformation):
    gy, gz = lax.axis_size("gy"), lax.axis_size("gz")
    owners = gy * gz
    _, ez, ey, lx = flow_state.shape
    cells = ez * ey
    me = lax.axis_index("gy") * gz + lax.axis_index("gz")

    state = flow_state.astype(jnp.float32)
    y_pad = halos(flow_state, "gy", 2, 3).astype(jnp.float32)
    z_pad = halos(flow_state, "gz", 1, 3).astype(jnp.float32)
    gx, gyy, gzz = diff_roll(state, 3), diff_pad(y_pad, 2), diff_pad(z_pad, 1)
    speeds, heat = state[:3], state[3]
    contra = [sum(metric[k, j] * speeds[k] for k in range(3)) for j in range(3)]
    carried = contra[0] * gx + contra[1] * gyy + contra[2] * gzz
    prov = []
    for c in range(3):
        change = -carried[c] - sum(deformation[c, l] * speeds[l] for l in range(3))
        if c == 2:
            change = change + heat
        prov.append(speeds[c] + substep_width * change)
    heat_next = heat + substep_width * (-carried[3] - speeds[2])

    flux = [sum(metric[c, j] * prov[c] for c in range(3)) for j in range(3)]
    div = (
        diff_roll(flux[0], 2)
        + diff_pad(halos(flux[1], "gy", 1, 3), 1)
        + diff_pad(halos(flux[2], "gz", 0, 3), 0)
    )

    cos_x, sin_x, weight = x_tables(lx)
    ahead = f32(by_owner(cos_x, sin_x, owners))
    back = f32(by_owner(cos_x * weight, sin_x * weight, owners))
    m = lx // 2 // owners
    spec = jnp.einsum("kx,rx->kr", ahead, div.reshape(cells, lx), precision=high)
    spec = lax.all_to_all(
        spec.reshape(owners, 2 * m, cells), ("gy", "gz"), split_axis=0, concat_axis=0, tiled=True
    )
    twist, kron, block, ky, kz, edge = plane_tables(gy, gz, ey, ez)
    tr, ti = f32(np.cos(twist))[:, None], f32(np.sin(twist))[:, None]
    wr, wi = f32(np.cos(kron)), f32(np.sin(kron))
    br, bi = f32(np.cos(block)), f32(np.sin(block))

    def ein(form, a, b):
        return jnp.einsum(form, a, b, precision=high)

    re, im = spec[:, :m], spec[:, m:]
    re, im = (
        ein("ts,smr->tmr", br, re) - ein("ts,smr->tmr", bi, im),
        ein("ts,smr->tmr", br, im) + ein("ts,smr->tmr", bi, re),
    )
    re, im = re * tr - im * ti, re * ti + im * tr
    re, im = (
        ein("tmr,rp->tmp", re, wr) - ein("tmr,rp->tmp", im, wi),
        ein("tmr,rp->tmp", im, wr) + ein("tmr,rp->tmp", re, wi),
    )
    modes = me * m + jnp.arange(m)
    kx = jnp.take(f32(wave(np.arange(lx // 2), lx)), modes)[None, :, None]
    ky, kz = f32(ky)[:, None], f32(kz)[:, None]
    symbol = sum((metric[c, 0] * kx + metric[c, 1] * ky + metric[c, 2] * kz) ** 2 for c in range(3))
    at_edge = jnp.asarray(edge)[:, None] & (modes == 0)[None, :, None]
    total = float(lx * ey * gy * ez * gz)
    factor = jnp.where(at_edge, 0.0, -1.0 / (jnp.where(at_edge, 1.0, symbol) * total))
    re, im = re * factor, im * factor
    re, im = (
        ein("tmr,rp->tmp", re, wr) + ein("tmr,rp->tmp", im, wi),
        ein("tmr,rp->tmp", im, wr) - ein("tmr,rp->tmp", re, wi),
    )
    re, im = re * tr + im * ti, im * tr - re * ti
    re, im = (
        ein("ts,smr->tmr", br, re) + ein("ts,smr->tmr", bi, im),
        ein("ts,smr->tmr", br, im) - ein("ts,smr->tmr", bi, re),
    )
    spec = lax.all_to_all(
        jnp.concatenate([re, im], axis=1), ("gy", "gz"), split_axis=0, concat_axis=0, tiled=True
    )
    pressure = jnp.einsum("kr,kx->rx", spec.reshape(lx, cells), back, precision=high)
    pressure = pressure.reshape(ez, ey, lx)
    push = [
        diff_roll(pressure, 2),
        diff_pad(halos(pressure, "gy", 1, 3), 1),
        diff_pad(halos(pressure, "gz", 0, 3), 0),
    ]
    motion = jnp.stack([prov[c] - sum(metric[c, j] * push[j] for j in range(3)) for c in range(3)])
    return motion, heat_next


def solution(mesh):
    placed = (P(None, "gz", "gy", None), P(), P())
    return jax.shard_map(
        shards,
        mesh=mesh,
        in_specs=placed,
        out_specs=(P(None, "gz", "gy", None), P("gz", "gy", None)),
        check_vma=False,
    )
```

profile of v0, /device:TPU:0, one launch (start us, length us, event | category | flops | bytes accessed | tf_op | source)
XLA Modules:
  0.0 152.1 jit_solution(6985839305062959454)
XLA Ops:
  0.6 3.0 %fusion.147 = (bf16[4,32,3,512]{3,2,1,0:T(4,128)(2,1)}, bf16[4,32,3,512]{3,2,1,0:T(4,128)(2,1)}) fusion(bf16[4,32,8,512]{3,2,1,0:T(8,128)(2,1)} %param.15), kind=kLoop, calls=%fused_computation.253 | loop fusion | bytes 1572864 | tf_op jit(solution)/shard_map/slice | solution.py:17
  3.6 3.0 %collective-permute-start = (bf16[4,32,3,512]{3,2,1,0:T(4,128)(2,1)}, bf16[4,32,3,512]{3,2,1,0:T(4,128)(2,1)}, u32[]{:S(2)}, u32[]{:S(2)}) collective-permute-start(bf16[4,32,3,512]{3,2,1,0:T(4,128)(2,1)} %get-tuple-element.31), channel_id=1, source_target_pairs={{0,4},{4,8},{8,12},{12,16},{16,20},{20,24},{24,28},{28,0},{1,5},{5... | collective-permute-start | bytes 1179656 | tf_op jit(solution)/shard_map/ppermute | solution.py:16
  6.6 3.0 %collective-permute-start.1 = (bf16[4,32,3,512]{3,2,1,0:T(4,128)(2,1)}, bf16[4,32,3,512]{3,2,1,0:T(4,128)(2,1)}, u32[]{:S(2)}, u32[]{:S(2)}) collective-permute-start(bf16[4,32,3,512]{3,2,1,0:T(4,128)(2,1)} %get-tuple-element.32), channel_id=1, source_target_pairs={{4,0},{8,4},{12,8},{16,12},{20,16},{24,20},{28,24},{0,28},{5,1},{9... | collective-permute-start | bytes 1179656 | tf_op jit(solution)/shard_map/ppermute | solution.py:19
  9.7 1.7 %collective-permute-start.3 = (bf16[4,3,8,512]{3,2,1,0:T(8,128)(2,1)S(1)}, bf16[4,3,8,512]{3,2,1,0:T(8,128)(2,1)}, u32[]{:S(2)}, u32[]{:S(2)}) collective-permute-start(bf16[4,3,8,512]{3,2,1,0:T(8,128)(2,1)S(1)} %get-tuple-element.34), channel_id=1, source_target_pairs={{1,0},{2,1},{3,2},{0,3},{5,4},{6,5},{7,6},{4,7},{9,8},{10,9},{11,1... | collective-permute-start | bytes 294920 | tf_op jit(solution)/shard_map/ppermute | solution.py:19
  11.5 0.3 convert_element_type.9
  11.8 2.6 %fusion.142 = (f32[4,32,8,509]{3,2,1,0:T(8,128)}, f32[4,32,8,509]{3,2,1,0:T(8,128)}) fusion(bf16[4,32,8,512]{3,2,1,0:T(8,128)(2,1)S(1)} %copy-done), kind=kLoop, calls=%fused_computation.248 | loop fusion | bytes 8339456 | tf_op jit(solution)/shard_map/jit(_roll_static)/slice | solution.py:30
  14.4 2.7 %fusion.144 = (f32[4,32,8,510]{3,2,1,0:T(8,128)}, f32[4,32,8,510]{3,2,1,0:T(8,128)}) fusion(bf16[4,32,8,512]{3,2,1,0:T(8,128)(2,1)S(1)} %copy-done), kind=kLoop, calls=%fused_computation.250 | loop fusion | bytes 8355840 | tf_op jit(solution)/shard_map/jit(_roll_static)/slice | solution.py:30
  17.1 2.8 %fusion.146 = (f32[4,32,8,511]{3,2,1,0:T(8,128)}, f32[4,32,8,511]{3,2,1,0:T(8,128)}) fusion(bf16[4,32,8,512]{3,2,1,0:T(8,128)(2,1)S(1)} %copy-done), kind=kLoop, calls=%fused_computation.252 | loop fusion | bytes 8372224 | tf_op jit(solution)/shard_map/jit(_roll_static)/slice | solution.py:30
  19.8 1.1 fusion.141
  21.0 1.1 fusion.143
  22.0 0.7 fusion.166
  22.7 7.1 %multiply_bitcast_fusion.2 = (f32[32,8,512]{2,1,0:T(8,128)}, f32[32,8,512]{2,1,0:T(8,128)}, f32[32,8,512]{2,1,0:T(8,128)}) fusion(f32[4,32,8,512]{3,2,1,0:T(8,128)S(1)} %convert_element_type.9, f32[]{:T(128)} %bitcast.3, f32[]{:T(128)} %bitcast.2, f32[]{:T(128)} %bitcast.1, f32[]{:T(128)} %bitcast.11, f32[]{:T(128)} %bitcast.10, f32[]{:T(128)} %bitcast.9, ...), kind=kLoop, calls=%fused_computation.192 | loop fusion | flops 2359296 | bytes 3145764 | tf_op jit(solution)/shard_map/mul | solution.py:97
  29.9 1.1 fusion.145
  31.0 0.7 fusion.165
  31.7 0.6 copy-done.12
  32.3 1.1 maximum_convert_fusion.1
  33.4 4.3 %maximum_convert_fusion = f32[4,32,14,512]{3,2,1,0:T(8,128)} fusion(bf16[4,32,3,512]{3,2,1,0:T(4,128)(2,1)} %collective-permute-done.1, bf16[4,32,8,512]{3,2,1,0:T(8,128)(2,1)S(1)} %copy-done, bf16[4,32,3,512]{3,2,1,0:T(4,128)(2,1)} %collective-permute-done), kind=kLoop, calls=%fused_computation.27 | loop fusion | flops 5505024 | bytes 5505024 | tf_op jit(solution)/shard_map/convert_element_type | solution.py:92
  37.7 17.8 %fusion.2 = f32[4,32,8,512]{3,2,1,0:T(8,128)} fusion(f32[4,38,8,512]{3,2,1,0:T(8,128)S(1)} %maximum_convert_fusion.1, f32[4,32,14,512]{3,2,1,0:T(8,128)} %maximum_convert_fusion, f32[4,32,8,1]{3,2,1,0:T(8,128)} %get-tuple-element.28, f32[4,32,8,511]{3,2,1,0:T(8,128)} %get-tuple-element.30, f32[4,32,8,511]{3,2,1,0:T(8,128)} %get-tuple-element.29, ...), kind=kLoop, calls=%fused_computation.4 | loop fusion | flops 16777216 | bytes 41418752 | tf_op jit(solution)/shard_map/add | solution.py:97
  55.6 9.9 %multiply_add_fusion.2 = (f32[32,8,512]{2,1,0:T(8,128)S(1)}, f32[32,8,512]{2,1,0:T(8,128)S(1)}, f32[32,8,512]{2,1,0:T(8,128)S(1)}, f32[32,8,512]{2,1,0:T(8,128)S(1)}) fusion(f32[]{:T(128)} %bitcast.3, f32[]{:T(128)} %bitcast.2, f32[]{:T(128)} %bitcast.1, f32[4,32,8,512]{3,2,1,0:T(8,128)} %copy-done.2, f32[]{:T(128)} %bitcast.17, f32[]{:T(128)} %bitcast.15, ...), kind=kLoop, calls=%fused_computation.189 | loop fusion | flops 4325376 | bytes 5767216 | tf_op jit(solution)/shard_map/add | solution.py:106
  66.4 4.1 %multiply_add_fusion.1 = (f32[32,8,512]{2,1,0:T(8,128)S(1)}, f32[32,8,512]{2,1,0:T(8,128)S(1)}) fusion(f32[32,8,512]{2,1,0:T(8,128)S(1)} %get-tuple-element.11, f32[32,8,512]{2,1,0:T(8,128)S(1)} %get-tuple-element.10, f32[32,8,512]{2,1,0:T(8,128)S(1)} %get-tuple-element.9, f32[]{:T(128)} %bitcast.7, f32[]{:T(128)} %bitcast.6, f32[]{:T(128)} %bitcast.5, ...), kind=kLoop, calls=%fused_computation.188 | loop fusion | flops 1310720 | bytes 2621464 | tf_op jit(solution)/shard_map/add | solution.py:106
  70.5 2.1 %collective-permute-start.4 = (f32[32,3,512]{2,1,0:T(4,128)S(1)}, f32[32,3,512]{2,1,0:T(4,128)S(1)}, u32[]{:S(2)}, u32[]{:S(2)}) collective-permute-start(f32[32,3,512]{2,1,0:T(4,128)S(1)} %get-tuple-element.67), channel_id=1, source_target_pairs={{4,0},{8,4},{12,8},{16,12},{20,16},{24,20},{28,24},{0,28},{5,1},{9... | collective-permute-start | bytes 589832 | tf_op jit(solution)/shard_map/ppermute | solution.py:19
  72.7 0.5 collective-permute-start.7
  73.3 1.1 collective-permute-done.6
  74.4 2.5 %collective-permute-done.7 = f32[3,8,512]{2,1,0:T(8,128)S(1)} collective-permute-done((f32[3,8,512]{2,1,0:T(8,128)S(1)}, f32[3,8,512]{2,1,0:T(8,128)S(1)}, u32[]{:S(2)}, u32[]{:S(2)}) %collective-permute-start.7) | collective-permute-done | bytes 49184 | tf_op jit(solution)/shard_map/ppermute | solution.py:16
  76.9 7.5 %collective-permute-done.4 = f32[32,3,512]{2,1,0:T(4,128)S(1)} collective-permute-done((f32[32,3,512]{2,1,0:T(4,128)S(1)}, f32[32,3,512]{2,1,0:T(4,128)S(1)}, u32[]{:S(2)}, u32[]{:S(2)}) %collective-permute-start.4) | collective-permute-done | bytes 196640 | tf_op jit(solution)/shard_map/ppermute | solution.py:19
  84.5 2.6 %fusion.102 = f32[512,256]{1,0:T(8,128)} fusion(f32[512,512]{1,0:T(8,128)S(1)} %copy-done.18, f32[32,8,512]{2,1,0:T(8,128)S(1)} %get-tuple-element.18, f32[3,8,512]{2,1,0:T(8,128)S(1)} %collective-permute-done.7, f32[3,8,512]{2,1,0:T(8,128)S(1)} %collective-permute-done.6, f32[32,8,512]{2,1,0:T(8,128)S(1)} %get-tuple-element.17, ...), kind=kOutput, calls=%fused_computation.193 | convolution fusion | flops 408158208 | bytes 6258688 | tf_op jit(solution)/shard_map/kx,rx->kr/dot_general | solution.py:117
  87.1 3.8 %all-to-all-start = ((f32[32,16,256]{2,1,0:T(8,128)}), f32[32,16,256]{2,1,0:T(8,128)S(1)}, u32[]{:S(2)}, u32[]{:S(2)}) async-start(f32[32,16,256]{2,1,0:T(8,128)} %bitcast.29), calls=%async_computation | async-start | bytes 1048576 | tf_op jit(solution)/shard_map/all_to_all | solution.py:118
  91.0 0.6 gather_fusion
  91.6 0.6 broadcast_multiply_fusion.8
  92.3 1.3 broadcast_multiply_fusion.7
  93.6 3.8 %broadcast_multiply_fusion.4 = (f32[32,256]{1,0:T(8,128)S(1)}, f32[32,256]{1,0:T(8,128)S(1)}, f32[32,256]{1,0:T(8,128)S(1)}, f32[32,256]{1,0:T(8,128)S(1)}, f32[32,256]{1,0:T(8,128)S(1)}, /*index=5*/f32[32,256]{1,0:T(8,128)S(1)}) fusion(f32[32,256]{1,0:T(8,128)S(1)} %copy-done.14, f32[]{:T(128)} %bitcast.9, f32[]{:T(128)} %bitcast.11, f32[]{:T(128)} %bitcast.10, ...), kind=kLoop, calls=%fused_computation.231 | loop fusion | flops 49152 | bytes 262168 | tf_op jit(solution)/shard_map/mul | solution.py:142
  97.4 9.0 %all-to-all-done = f32[32,16,256]{2,1,0:T(8,128)S(1)} async-done(((f32[32,16,256]{2,1,0:T(8,128)}), f32[32,16,256]{2,1,0:T(8,128)S(1)}, u32[]{:S(2)}, u32[]{:S(2)}) %all-to-all-start) | async-done | bytes 524320 | tf_op jit(solution)/shard_map/all_to_all | solution.py:118
  106.5 0.3 fusion.113
  106.8 0.3 fusion.109
  107.1 0.3 fusion.22
  107.4 0.3 multiply_add_fusion.4
  107.8 0.4 fusion.121
  108.2 0.4 fusion.125
  108.6 0.5 fusion.19
  109.0 0.3 fusion.115
  109.4 0.5 fusion.20
  109.8 0.3 fusion.119
  110.1 0.3 convolution_subtract_fusion.1
  110.5 0.3 convolution_add_fusion.1
  110.8 0.3 fusion.127
  111.1 0.3 fusion.128
  111.3 0.3 fusion.18
  111.6 0.3 fusion.17
  111.9 1.1 copy.46
  113.0 3.3 %all-to-all-start.1 = ((f32[32,16,256]{2,1,0:T(8,128)}), f32[32,16,256]{2,1,0:T(8,128)}, u32[]{:S(2)}, u32[]{:S(2)}) async-start(f32[32,16,256]{2,1,0:T(8,128)} %copy.46), calls=%async_computation.1 | async-start | bytes 1048576 | tf_op jit(solution)/shard_map/all_to_all | solution.py:156
  122.1 2.0 %fusion.70 = f32[32,8,512]{2,1,0:T(8,128)} fusion(f32[4,32,8,512]{3,2,1,0:T(8,128)} %fusion.2, f32[4,32,8,512]{3,2,1,0:T(8,128)S(1)} %copy-done.3), kind=kLoop, calls=%fused_computation.124 | loop fusion | flops 524288 | bytes 2097152 | tf_op jit(solution)/shard_map/add | solution.py:104
  124.1 7.8 %all-to-all-done.1 = f32[32,16,256]{2,1,0:T(8,128)} async-done(((f32[32,16,256]{2,1,0:T(8,128)}), f32[32,16,256]{2,1,0:T(8,128)}, u32[]{:S(2)}, u32[]{:S(2)}) %all-to-all-start.1) | async-done | bytes 524320 | tf_op jit(solution)/shard_map/all_to_all | solution.py:156
  131.9 2.0 %fusion.167 = f32[256,512]{1,0:T(8,128)S(1)} fusion(f32[512,256]{1,0:T(8,128)} %bitcast.39, f32[512,512]{1,0:T(8,128)} %constant.83.clone), kind=kOutput, calls=%fused_computation.273 | convolution fusion | flops 402653184 | bytes 2097152 | tf_op jit(solution)/shard_map/kr,kx->rx/dot_general | solution.py:159
  134.1 0.2 fusion.152
  134.3 0.2 fusion.154
  134.8 1.7 %collective-permute-start.8 = (f32[32,3,512]{2,1,0:T(4,128)S(1)}, f32[32,3,512]{2,1,0:T(4,128)S(1)}, u32[]{:S(2)}, u32[]{:S(2)}) collective-permute-start(f32[32,3,512]{2,1,0:T(4,128)S(1)} %get-tuple-element.39), channel_id=1, source_target_pairs={{4,0},{8,4},{12,8},{16,12},{20,16},{24,20},{28,24},{0,28},{5,1},{9... | collective-permute-start | bytes 589832 | tf_op jit(solution)/shard_map/ppermute | solution.py:19
  136.6 0.3 collective-permute-start.9
  136.9 0.4 collective-permute-start.10
  137.5 1.7 %collective-permute-done.10 = f32[3,8,512]{2,1,0:T(8,128)S(1)} collective-permute-done((f32[3,8,512]{2,1,0:T(8,128)S(1)}, f32[3,8,512]{2,1,0:T(8,128)S(1)}, u32[]{:S(2)}, u32[]{:S(2)}) %collective-permute-start.10) | collective-permute-done | bytes 49184 | tf_op jit(solution)/shard_map/ppermute | solution.py:19
  139.3 1.6 %collective-permute-done.11 = f32[3,8,512]{2,1,0:T(8,128)S(1)} collective-permute-done((f32[3,8,512]{2,1,0:T(8,128)S(1)}, f32[3,8,512]{2,1,0:T(8,128)S(1)}, u32[]{:S(2)}, u32[]{:S(2)}) %collective-permute-start.11) | collective-permute-done | bytes 49184 | tf_op jit(solution)/shard_map/ppermute | solution.py:16
  140.8 7.8 %collective-permute-done.8 = f32[32,3,512]{2,1,0:T(4,128)S(1)} collective-permute-done((f32[32,3,512]{2,1,0:T(4,128)S(1)}, f32[32,3,512]{2,1,0:T(4,128)S(1)}, u32[]{:S(2)}, u32[]{:S(2)}) %collective-permute-start.8) | collective-permute-done | bytes 196640 | tf_op jit(solution)/shard_map/ppermute | solution.py:19
  148.6 1.9 %subtract_bitcast_fusion.2 = (f32[1,32,8,512]{3,2,1,0:T(8,128)S(1)}, f32[32,8,512]{2,1,0:T(8,128)S(1)}, f32[32,8,512]{2,1,0:T(8,128)S(1)}, f32[32,8,512]{2,1,0:T(8,128)S(1)}) fusion(f32[32,8,512]{2,1,0:T(8,128)S(1)} %get-tuple-element.9, f32[]{:T(128)S(6)} %mul.623, f32[]{:T(128)S(6)} %mul.618, f32[]{:T(128)S(6)} %mul.613, ...), kind=kLoop, calls=%fused_computation.186 | loop fusion | flops 5898240 | bytes 6782988 | tf_op jit(solution)/shard_map/stack | solution.py:166
  150.6 0.3 subtract_bitcast_fusion.1
  150.9 1.3 pad_maximum_fusion
  (68 shorter events, 2.1 us)
Async XLA Ops:
  0.6 9.0 %copy-start = (bf16[4,32,8,512]{3,2,1,0:T(8,128)(2,1)S(1)}, bf16[4,32,8,512]{3,2,1,0:T(8,128)(2,1)}, u32[]{:S(2)}) copy-start(bf16[4,32,8,512]{3,2,1,0:T(8,128)(2,1)} %param.15) | copy-start | bytes 3145732
  3.6 29.8 %collective-permute-start = (bf16[4,32,3,512]{3,2,1,0:T(4,128)(2,1)}, bf16[4,32,3,512]{3,2,1,0:T(4,128)(2,1)}, u32[]{:S(2)}, u32[]{:S(2)}) collective-permute-start(bf16[4,32,3,512]{3,2,1,0:T(4,128)(2,1)} %get-tuple-element.31), channel_id=1, source_target_pairs={{0,4},{4,8},{8,12},{12,16},{16,20},{20,24},{24,28},{28,0},{1,5},{5... | collective-permute-start | bytes 1179656 | tf_op jit(solution)/shard_map/ppermute | solution.py:16
  6.6 26.8 %collective-permute-start.1 = (bf16[4,32,3,512]{3,2,1,0:T(4,128)(2,1)}, bf16[4,32,3,512]{3,2,1,0:T(4,128)(2,1)}, u32[]{:S(2)}, u32[]{:S(2)}) collective-permute-start(bf16[4,32,3,512]{3,2,1,0:T(4,128)(2,1)} %get-tuple-element.32), channel_id=1, source_target_pairs={{4,0},{8,4},{12,8},{16,12},{20,16},{24,20},{28,24},{0,28},{5,1},{9... | collective-permute-start | bytes 1179656 | tf_op jit(solution)/shard_map/ppermute | solution.py:19
  9.7 22.0 %collective-permute-start.2 = (bf16[4,3,8,512]{3,2,1,0:T(8,128)(2,1)S(1)}, bf16[4,3,8,512]{3,2,1,0:T(8,128)(2,1)S(1)}, u32[]{:S(2)}, u32[]{:S(2)}) collective-permute-start(bf16[4,3,8,512]{3,2,1,0:T(8,128)(2,1)S(1)} %get-tuple-element.33), channel_id=1, source_target_pairs={{0,1},{1,2},{2,3},{3,0},{4,5},{5,6},{6,7},{7,4},{8,9},{9,10},{10,1... | collective-permute-start | bytes 294920 | tf_op jit(solution)/shard_map/ppermute | solution.py:16
  9.7 22.6 %collective-permute-start.3 = (bf16[4,3,8,512]{3,2,1,0:T(8,128)(2,1)S(1)}, bf16[4,3,8,512]{3,2,1,0:T(8,128)(2,1)}, u32[]{:S(2)}, u32[]{:S(2)}) collective-permute-start(bf16[4,3,8,512]{3,2,1,0:T(8,128)(2,1)S(1)} %get-tuple-element.34), channel_id=1, source_target_pairs={{1,0},{2,1},{3,2},{0,3},{5,4},{6,5},{7,6},{4,7},{9,8},{10,9},{11,1... | collective-permute-start | bytes 294920 | tf_op jit(solution)/shard_map/ppermute | solution.py:19
  11.8 11.0 %copy-start.2 = (f32[4,32,8,512]{3,2,1,0:T(8,128)}, f32[4,32,8,512]{3,2,1,0:T(8,128)S(1)}, u32[]{:S(2)}) copy-start(f32[4,32,8,512]{3,2,1,0:T(8,128)S(1)} %convert_element_type.9) | copy-start | bytes 6291460
  19.8 2.2 %copy-start.15 = (f32[3,3]{1,0:T(4,128)S(1)}, f32[3,3]{1,0:T(4,128)}, u32[]{:S(2)}) copy-start(f32[3,3]{1,0:T(4,128)} %param.16) | copy-start | bytes 112
  22.7 8.2 %copy-start.16 = (f32[3,3]{1,0:T(4,128)S(1)}, f32[3,3]{1,0:T(4,128)}, u32[]{:S(2)}) copy-start(f32[3,3]{1,0:T(4,128)} %param.17) | copy-start | bytes 112
  31.7 0.6 copy-start.12
  65.5 0.9 copy-start.4
  66.3 18.1 %copy-start.18 = (f32[512,512]{1,0:T(8,128)S(1)}, f32[512,512]{1,0:T(8,128)}, u32[]{:S(2)}) copy-start(f32[512,512]{1,0:T(8,128)} %constant.82.clone) | copy-start | bytes 3145732
  70.5 13.9 %collective-permute-start.4 = (f32[32,3,512]{2,1,0:T(4,128)S(1)}, f32[32,3,512]{2,1,0:T(4,128)S(1)}, u32[]{:S(2)}, u32[]{:S(2)}) collective-permute-start(f32[32,3,512]{2,1,0:T(4,128)S(1)} %get-tuple-element.67), channel_id=1, source_target_pairs={{4,0},{8,4},{12,8},{16,12},{20,16},{24,20},{28,24},{0,28},{5,1},{9... | collective-permute-start | bytes 589832 | tf_op jit(solution)/shard_map/ppermute | solution.py:19
  72.6 11.8 %collective-permute-start.5 = (f32[32,3,512]{2,1,0:T(4,128)S(1)}, f32[32,3,512]{2,1,0:T(4,128)S(1)}, u32[]{:S(2)}, u32[]{:S(2)}) collective-permute-start(f32[32,3,512]{2,1,0:T(4,128)S(1)} %get-tuple-element.68), channel_id=1, source_target_pairs={{0,4},{4,8},{8,12},{12,16},{16,20},{20,24},{24,28},{28,0},{1,5},{5... | collective-permute-start | bytes 589832 | tf_op jit(solution)/shard_map/ppermute | solution.py:16
  72.6 1.8 %collective-permute-start.6 = (f32[3,8,512]{2,1,0:T(8,128)S(1)}, f32[3,8,512]{2,1,0:T(8,128)S(1)}, u32[]{:S(2)}, u32[]{:S(2)}) collective-permute-start(f32[3,8,512]{2,1,0:T(8,128)S(1)} %get-tuple-element.69), channel_id=1, source_target_pairs={{1,0},{2,1},{3,2},{0,3},{5,4},{6,5},{7,6},{4,7},{9,8},{10,9},{11,1... | collective-permute-start | bytes 147464 | tf_op jit(solution)/shard_map/ppermute | solution.py:19
  72.7 4.2 %collective-permute-start.7 = (f32[3,8,512]{2,1,0:T(8,128)S(1)}, f32[3,8,512]{2,1,0:T(8,128)S(1)}, u32[]{:S(2)}, u32[]{:S(2)}) collective-permute-start(f32[3,8,512]{2,1,0:T(8,128)S(1)} %get-tuple-element.70), channel_id=1, source_target_pairs={{0,1},{1,2},{2,3},{3,0},{4,5},{5,6},{6,7},{7,4},{8,9},{9,10},{10,1... | collective-permute-start | bytes 147464 | tf_op jit(solution)/shard_map/ppermute | solution.py:16
  84.4 6.5 %copy-start.17 = (pred[32,256]{1,0:T(32,128)(4,1)S(1)}, pred[32,256]{1,0:T(32,128)(4,1)}, u32[]{:S(2)}) copy-start(pred[32,256]{1,0:T(32,128)(4,1)} %constant.93.clone) | copy-start | bytes 24580
  84.4 6.5 %copy-start.1 = (f32[256]{0:T(256)S(1)}, f32[256]{0:T(256)}, u32[]{:S(2)}) copy-start(f32[256]{0:T(256)} %constant.90.clone) | copy-start | bytes 3076
  84.5 9.1 %copy-start.13 = (f32[32,256]{1,0:T(8,128)S(1)}, f32[32,256]{1,0:T(8,128)}, u32[]{:S(2)}) copy-start(f32[32,256]{1,0:T(8,128)} %constant.91.clone) | copy-start | bytes 98308
  84.5 9.1 %copy-start.14 = (f32[32,256]{1,0:T(8,128)S(1)}, f32[32,256]{1,0:T(8,128)}, u32[]{:S(2)}) copy-start(f32[32,256]{1,0:T(8,128)} %constant.92.clone) | copy-start | bytes 98308
  87.1 19.4 %copy-start.11 = (f32[32,32,1]{1,0,2:T(8,128)S(1)}, f32[32,32,1]{1,0,2:T(8,128)}, u32[]{:S(2)}) copy-start(f32[32,32,1]{1,0,2:T(8,128)} %constant.94) | copy-start | bytes 12292
  87.1 20.0 %copy-start.10 = (f32[32,32,1]{1,0,2:T(8,128)S(1)}, f32[32,32,1]{1,0,2:T(8,128)}, u32[]{:S(2)}) copy-start(f32[32,32,1]{1,0,2:T(8,128)} %constant.95) | copy-start | bytes 12292
  87.1 19.4 %all-to-all-start = ((f32[32,16,256]{2,1,0:T(8,128)}), f32[32,16,256]{2,1,0:T(8,128)S(1)}, u32[]{:S(2)}, u32[]{:S(2)}) async-start(f32[32,16,256]{2,1,0:T(8,128)} %bitcast.29), calls=%async_computation | async-start | bytes 1048576 | tf_op jit(solution)/shard_map/all_to_all | solution.py:118
  90.9 16.5 %copy-start.8 = (f32[32,256]{1,0:T(8,128)S(1)}, f32[32,256]{1,0:T(8,128)}, u32[]{:S(2)}) copy-start(f32[32,256]{1,0:T(8,128)} %constant.84.clone) | copy-start | bytes 98308
  90.9 16.5 %copy-start.9 = (f32[32,256]{1,0:T(8,128)S(1)}, f32[32,256]{1,0:T(8,128)}, u32[]{:S(2)}) copy-start(f32[32,256]{1,0:T(8,128)} %constant.85.clone) | copy-start | bytes 98308
  97.4 10.3 %copy-start.6 = (f32[256,256,1]{1,0,2:T(8,128)S(1)}, f32[256,256,1]{1,0,2:T(8,128)}, u32[]{:S(2)}) copy-start(f32[256,256,1]{1,0,2:T(8,128)} %constant.96) | copy-start | bytes 786436
  106.8 1.8 %copy-start.7 = (f32[256,256,1]{1,0,2:T(8,128)S(1)}, f32[256,256,1]{1,0,2:T(8,128)}, u32[]{:S(2)}) copy-start(f32[256,256,1]{1,0,2:T(8,128)} %constant.97) | copy-start | bytes 786436
  111.6 10.5 %copy-start.3 = (f32[4,32,8,512]{3,2,1,0:T(8,128)S(1)}, f32[4,32,8,512]{3,2,1,0:T(8,128)}, u32[]{:S(2)}) copy-start(f32[4,32,8,512]{3,2,1,0:T(8,128)} %copy-done.2) | copy-start | bytes 6291460
  113.0 18.9 %all-to-all-start.1 = ((f32[32,16,256]{2,1,0:T(8,128)}), f32[32,16,256]{2,1,0:T(8,128)}, u32[]{:S(2)}, u32[]{:S(2)}) async-start(f32[32,16,256]{2,1,0:T(8,128)} %copy.46), calls=%async_computation.1 | async-start | bytes 1048576 | tf_op jit(solution)/shard_map/all_to_all | solution.py:156
  134.8 13.8 %collective-permute-start.8 = (f32[32,3,512]{2,1,0:T(4,128)S(1)}, f32[32,3,512]{2,1,0:T(4,128)S(1)}, u32[]{:S(2)}, u32[]{:S(2)}) collective-permute-start(f32[32,3,512]{2,1,0:T(4,128)S(1)} %get-tuple-element.39), channel_id=1, source_target_pairs={{4,0},{8,4},{12,8},{16,12},{20,16},{24,20},{28,24},{0,28},{5,1},{9... | collective-permute-start | bytes 589832 | tf_op jit(solution)/shard_map/ppermute | solution.py:19
  136.6 12.0 %collective-permute-start.9 = (f32[32,3,512]{2,1,0:T(4,128)S(1)}, f32[32,3,512]{2,1,0:T(4,128)S(1)}, u32[]{:S(2)}, u32[]{:S(2)}) collective-permute-start(f32[32,3,512]{2,1,0:T(4,128)S(1)} %get-tuple-element.40), channel_id=1, source_target_pairs={{0,4},{4,8},{8,12},{12,16},{16,20},{20,24},{24,28},{28,0},{1,5},{5... | collective-permute-start | bytes 589832 | tf_op jit(solution)/shard_map/ppermute | solution.py:16
  136.9 2.3 %collective-permute-start.10 = (f32[3,8,512]{2,1,0:T(8,128)S(1)}, f32[3,8,512]{2,1,0:T(8,128)S(1)}, u32[]{:S(2)}, u32[]{:S(2)}) collective-permute-start(f32[3,8,512]{2,1,0:T(8,128)S(1)} %get-tuple-element.37), channel_id=1, source_target_pairs={{1,0},{2,1},{3,2},{0,3},{5,4},{6,5},{7,6},{4,7},{9,8},{10,9},{11,1... | collective-permute-start | bytes 147464 | tf_op jit(solution)/shard_map/ppermute | solution.py:19
  137.3 3.5 %collective-permute-start.11 = (f32[3,8,512]{2,1,0:T(8,128)S(1)}, f32[3,8,512]{2,1,0:T(8,128)S(1)}, u32[]{:S(2)}, u32[]{:S(2)}) collective-permute-start(f32[3,8,512]{2,1,0:T(8,128)S(1)} %get-tuple-element.38), channel_id=1, source_target_pairs={{0,1},{1,2},{2,3},{3,0},{4,5},{5,6},{6,7},{7,4},{8,9},{9,10},{10,1... | collective-permute-start | bytes 147464 | tf_op jit(solution)/shard_map/ppermute | solution.py:16
  148.6 1.9 %copy-start.5 = (f32[32,8,512]{2,1,0:T(8,128)S(1)}, f32[32,8,512]{2,1,0:T(8,128)}, u32[]{:S(2)}) copy-start(f32[32,8,512]{2,1,0:T(8,128)} %copy-done.4) | copy-start | bytes 1572868
where the time goes:
time: 153 us; the launch traced here: 152 us
  other arithmetic  55.9 us (37%)
  waiting for transfers between devices  39.1 us (26%)
  local copies, waits for them, and re-layouts  20.3 us (13%)
  starting transfers between devices  20.2 us (13%)
  matrix products  9.79 us (6%)
  between operations  6.93 us (5%)
    ppermute x6, waiting for transfers between devices, halos(): lax.ppermute(lax.slice_in_dim(block, 0, width, axis=dim), axis, backward)  18.2 us
    add x1, other arithmetic, shards(): carried = contra[0] * gx + contra[1] * gyy + contra[2] * gzz  17.8 us
    add x2, other arithmetic, shards(): flux = [sum((metric[c, j] * prov[c] for c in range(3))) for j in range(3)]  14 us
    slice x18, local copies, waits for them, and re-layouts, diff_roll(): return stencil(lambda offset: jnp.roll(f, -offset, axis=along))  13.2 us
    ppermute x6, starting transfers between devices, halos(): lax.ppermute(lax.slice_in_dim(block, 0, width, axis=dim), axis, backward)  9.04 us
    all_to_all x1, waiting for transfers between devices, shards(): lax.all_to_all(spec.reshape(owners, 2 * m, cells), ('gy', 'gz'), split_ax...  8.99 us
    all_to_all x1, waiting for transfers between devices, shards(): lax.all_to_all(jnp.concatenate([re, im], axis=1), ('gy', 'gz'), split_axi...  7.79 us
    mul x1, other arithmetic, shards(): carried = contra[0] * gx + contra[1] * gyy + contra[2] * gzz  7.13 us
  transfers between devices with their start and end apart: 14, of which 8 were waited for; matrix products, arithmetic and copies ran while one was open for 20% of the time, Pallas kernels for 0%

commit v1 on v0

v1 whole, which is shorter than its diff:
```python
import numpy as np

import jax
import jax.numpy as jnp
from jax import lax
from jax.experimental import pallas as pl
from jax.experimental.pallas import tpu as pltpu
from jax.sharding import PartitionSpec as P

substep_width = 0.4
mesh_ids = pl.DeviceIdType.MESH
coefs = {1: 45.0, 2: -9.0, 3: 1.0, -1: -45.0, -2: 9.0, -3: -1.0}


def x_tables(length):
    half = length // 2
    k = np.arange(half)[:, None]
    x = np.arange(length)[None, :]
    angle = 2.0 * np.pi * ((k * x) % length) / length
    c, s = np.cos(angle), -np.sin(angle)
    s[0] = np.where(np.arange(length) % 2 == 0, 1.0, -1.0)
    weight = np.where(np.arange(half) == 0, 1.0, 2.0)[:, None]
    return c, s, weight


def by_owner(re, im, owners):
    half, length = re.shape
    m = half // owners
    return np.concatenate(
        [re.reshape(owners, m, length), im.reshape(owners, m, length)], axis=1
    ).reshape(2 * half, length)


def wave(m, length):
    a = 2.0 * np.pi * m / length
    value = 1.5 * np.sin(a) - 0.3 * np.sin(2 * a) + np.sin(3 * a) / 30.0
    return np.where((2 * m) % length == 0, 0.0, value)


def plane_tables(gy, gz, ey, ez):
    ly, lz = gy * ey, gz * ez
    b = np.repeat(np.arange(ez), ey)
    e = np.tile(np.arange(ey), ez)
    s = np.repeat(np.arange(gy), gz)[:, None]
    q = np.tile(np.arange(gz), gy)[:, None]
    twist = -2.0 * np.pi * (b * q / lz + e * s / ly)
    kron = -2.0 * np.pi * (np.outer(b, b) / ez + np.outer(e, e) / ey)
    my = gy * e[None, :] + s
    mz = gz * b[None, :] + q
    block = -2.0 * np.pi * (
        np.outer(s, s) / gy + np.outer(q, q) / gz
    )
    edge = ((2 * my) % ly == 0) & ((2 * mz) % lz == 0)
    return twist, kron, block, wave(my, ly), wave(mz, lz), edge


def stencil_tables(ez, ey, lx):
    cells = ez * ey
    own = np.zeros((2 * cells, cells))
    beside = np.zeros((2 * cells, 6 * ez + 8 * ey))
    pick = np.zeros((6 * ez, cells))
    for z in range(ez):
        for y in range(ey):
            r = z * ey + y
            for o, w in coefs.items():
                t = y + o
                if 0 <= t < ey:
                    own[r, z * ey + t] += w
                elif t < 0:
                    beside[r, (t + 3) * ez + z] += w
                else:
                    beside[r, (3 + t - ey) * ez + z] += w
                t = z + o
                if 0 <= t < ez:
                    own[cells + r, t * ey + y] += w
                elif t < 0:
                    beside[cells + r, 6 * ez + (t + 4) * ey + y] += w
                else:
                    beside[cells + r, 6 * ez + 4 * ey + (t - ez) * ey + y] += w
        for j in range(3):
            pick[j * ez + z, z * ey + ey - 3 + j] = 1.0
            pick[(3 + j) * ez + z, z * ey + j] = 1.0
    along_x = np.zeros((lx, lx))
    for o, w in coefs.items():
        x = np.arange(lx)
        along_x[(x + o) % lx, x] += w
    return own, beside, pick, along_x


def halves(a):
    a = np.asarray(a, np.float32)
    top = a.astype(jnp.bfloat16)
    return [top, (a - top.astype(np.float32)).astype(jnp.bfloat16)]


def split(x, pieces=2):
    out = []
    for _ in range(pieces):
        top = x.astype(jnp.bfloat16)
        out.append(top)
        x = x - top.astype(jnp.float32)
    return out


def dot(a, b, ca=1, cb=0):
    return lax.dot_general(a, b, (((ca,), (cb,)), ((), ())), preferred_element_type=jnp.float32)


def dot3(a, b, ca=1, cb=0):
    return dot(a[0], b[0], ca, cb) + dot(a[0], b[1], ca, cb) + dot(a[1], b[0], ca, cb)


def kernel(
    sizes, metric, deform, state, own, beside, beside_sum, pick, along_x, big_hbm, plane_hbm,
    motion, heat_next,
    big, plane, edge_state, halo_state, grad, grad_x, prov, flux, edge_f, halo_f, div,
    edge_p, halo_p, press, line, there, here, there2, here2, factor,
    load_sem, s_send, s_recv, f_send, f_recv, p_send, p_recv, a_send, a_recv, b_send, b_recv,
):
    gy, gz, ez, ey, lx = sizes
    owners = gy * gz
    cells = ez * ey
    rows2 = lx // owners
    m = rows2 // 2
    ye, ze = 3 * ez, 4 * ey
    iy, iz = lax.axis_index("gy"), lax.axis_index("gz")
    me = iy * gz + iz
    up_y = (lax.rem(iy + 1, gy), iz)
    down_y = (lax.rem(iy + gy - 1, gy), iz)
    up_z = (iy, lax.rem(iz + 1, gz))
    down_z = (iy, lax.rem(iz + gz - 1, gz))

    load_big = pltpu.make_async_copy(big_hbm, big, load_sem.at[0])
    load_plane = pltpu.make_async_copy(plane_hbm, plane, load_sem.at[1])
    load_big.start()
    load_plane.start()

    barrier = pltpu.get_barrier_semaphore()

    def greet(i, carry):
        other = lax.rem(me + i, owners)
        pl.semaphore_signal(
            barrier, inc=1, device_id=(other // gz, lax.rem(other, gz)), device_id_type=mesh_ids
        )
        return carry

    lax.fori_loop(1, owners, greet, 0)

    for c in range(4):
        picked = dot(pick[...], state[c]).astype(jnp.bfloat16)
        edge_state[0, c] = picked[:ye]
        edge_state[1, c] = picked[ye:]
    pl.semaphore_wait(barrier, owners - 1)

    def send(src, dst, send_sem, recv_sem, to):
        copy = pltpu.make_async_remote_copy(
            src_ref=src, dst_ref=dst, send_sem=send_sem, recv_sem=recv_sem,
            device_id=to, device_id_type=mesh_ids,
        )
        copy.start()
        return copy

    halo_copies = [
        send(edge_state.at[0], halo_state.at[:, 0:ye], s_send.at[0], s_recv.at[0], up_y),
        send(edge_state.at[1], halo_state.at[:, ye : 2 * ye], s_send.at[1], s_recv.at[1], down_y),
        send(
            state.at[:, cells - ze : cells], halo_state.at[:, 2 * ye : 2 * ye + ze],
            s_send.at[2], s_recv.at[2], up_z,
        ),
        send(
            state.at[:, 0:ze], halo_state.at[:, 2 * ye + ze : 2 * ye + 2 * ze],
            s_send.at[3], s_recv.at[3], down_z,
        ),
    ]
    for c in range(4):
        grad[c] = dot(own[...], state[c])
        grad_x[c] = dot(state[c], along_x[...])
    for copy in halo_copies:
        copy.wait()
    for c in range(4):
        grad[c] += dot(beside[...], halo_state[c])

    sixtieth = 1.0 / 60.0

    def advance(i, carry):
        rows = pl.ds(pl.multiple_of(i * 16, 16), 16)
        rows_z = pl.ds(pl.multiple_of(cells + i * 16, 16), 16)
        f = [state[c, rows, :].astype(jnp.float32) for c in range(4)]
        contra = [
            (metric[0, j] * f[0] + metric[1, j] * f[1] + metric[2, j] * f[2]) * sixtieth
            for j in range(3)
        ]
        carried = [
            contra[0] * grad_x[c, rows, :]
            + contra[1] * grad[c, rows, :]
            + contra[2] * grad[c, rows_z, :]
            for c in range(4)
        ]
        new = []
        for c in range(3):
            change = -carried[c] - (
                deform[c, 0] * f[0] + deform[c, 1] * f[1] + deform[c, 2] * f[2]
            )
            if c == 2:
                change = change + f[3]
            new.append(f[c] + substep_width * change)
            prov[c, rows, :] = new[c]
        heat_next[rows, :] = f[3] + substep_width * (-carried[3] - f[2])
        for j in range(3):
            flux[j, rows, :] = metric[0, j] * new[0] + metric[1, j] * new[1] + metric[2, j] * new[2]
        return carry

    lax.fori_loop(0, cells // 16, advance, 0)

    f1 = split(flux[1])
    f2 = split(flux[2])
    edge_f[...] = dot(pick[...], f1[0]) + dot(pick[...], f1[1])
    halo_copies = [
        send(edge_f.at[0:ye], halo_f.at[0:ye], f_send.at[0], f_recv.at[0], up_y),
        send(edge_f.at[ye : 2 * ye], halo_f.at[ye : 2 * ye], f_send.at[1], f_recv.at[1], down_y),
        send(
            flux.at[2, cells - ze : cells], halo_f.at[2 * ye : 2 * ye + ze],
            f_send.at[2], f_recv.at[2], up_z,
        ),
        send(
            flux.at[2, 0:ze], halo_f.at[2 * ye + ze : 2 * ye + 2 * ze],
            f_send.at[3], f_recv.at[3], down_z,
        ),
    ]
    f0 = split(flux[0])
    div[...] = (
        dot(f0[0], along_x[...]) + dot(f0[1], along_x[...])
        + dot(own[0:cells], f1[0]) + dot(own[0:cells], f1[1])
        + dot(own[cells:], f2[0]) + dot(own[cells:], f2[1])
    )
    load_big.wait()
    load_plane.wait()
    for copy in halo_copies:
        copy.wait()
    h = split(halo_f[...])
    d = split((div[...] + dot(beside_sum[...], h[0]) + dot(beside_sum[...], h[1])) * sixtieth)

    def spread(buffer):
        if rows2 % 8 == 0:
            buffer[...] = line[...].reshape(owners, rows2, cells)
        else:
            for k in range(owners):
                buffer[k] = line[k * rows2 : (k + 1) * rows2, :]

    def gather(buffer):
        if rows2 % 8 == 0:
            return buffer[...].reshape(owners * rows2, cells)
        for k in range(owners):
            line[k * rows2 : (k + 1) * rows2, :] = buffer[k]
        return line[...]

    def exchange(source, target, send_sem, recv_sem, meanwhile):
        def copy_of(i):
            other = lax.rem(me + i, owners)
            return pltpu.make_async_remote_copy(
                src_ref=source.at[other], dst_ref=target.at[me],
                send_sem=send_sem.at[i], recv_sem=recv_sem.at[i],
                device_id=(other // gz, lax.rem(other, gz)), device_id_type=mesh_ids,
            )

        def begin(i, carry):
            copy_of(i).start()
            return carry

        def end(i, carry):
            copy_of(i).wait()
            return carry

        lax.fori_loop(1, owners, begin, 0)
        target[me] = source[me]
        meanwhile()
        lax.fori_loop(1, owners, end, 0)

    def make_factor():
        row = lax.broadcasted_iota(jnp.int32, (2 * m * owners // 2, cells), 0)
        mode = me * m + (row & (m - 1))
        u = (mode - lx // 4).astype(jnp.float32) * (2.0 * np.pi / lx)
        v = u * u
        sine = jnp.zeros_like(u)
        cosine = jnp.zeros_like(u)
        for n in range(9, -1, -1):
            sign = -1.0 if n % 2 else 1.0
            sine = sine * v + sign / float(np.prod(np.arange(1.0, 2 * n + 1)))
            cosine = cosine * v + sign / float(np.prod(np.arange(1.0, 2 * n + 2)))
        cosine = -u * cosine
        kx = (
            1.5 * sine - 0.6 * sine * cosine + sine * (3.0 - 4.0 * sine * sine) * (1.0 / 30.0)
        )
        zero_mode = mode == 0
        kx = jnp.where(zero_mode, 0.0, kx)
        ky, kz = plane[2], plane[3]
        symbol = jnp.zeros_like(kx)
        for c in range(3):
            mixed = metric[c, 0] * kx + metric[c, 1] * ky + metric[c, 2] * kz
            symbol = symbol + mixed * mixed
        at_edge = zero_mode & (plane[4] > 0.5)
        total = float(lx * ey * gy * ez * gz)
        factor[...] = jnp.where(at_edge, 0.0, -1.0 / (jnp.where(at_edge, 1.0, symbol) * total))

    line[...] = dot3((big[0], big[1]), d, 1, 1)
    spread(there)
    exchange(there, here, a_send, a_recv, make_factor)

    half = lx // 2
    out = dot3((big[4], big[5]), split(gather(here)))
    re, im = out[:half], out[half:]
    tr, ti = plane[0], plane[1]
    both = jnp.concatenate([re * tr - im * ti, re * ti + im * tr], axis=1)
    out = dot3(split(both), (big[8], big[9]))
    re, im = out[:, :cells] * factor[...], out[:, cells:] * factor[...]
    both = jnp.concatenate([re, im], axis=1)
    out = dot3(split(both), (big[10], big[11]))
    re, im = out[:, :cells], out[:, cells:]
    both = jnp.concatenate([re * tr + im * ti, im * tr - re * ti], axis=0)
    line[...] = dot3((big[6], big[7]), split(both))
    spread(there2)
    exchange(there2, here2, b_send, b_recv, lambda: None)

    press[...] = dot3(split(gather(here2)), (big[2], big[3]), 0, 0)
    p = split(press[...], 3)
    edge_p[...] = dot(pick[...], p[0]) + dot(pick[...], p[1]) + dot(pick[...], p[2])
    halo_copies = [
        send(edge_p.at[0:ye], halo_p.at[0:ye], p_send.at[0], p_recv.at[0], up_y),
        send(edge_p.at[ye : 2 * ye], halo_p.at[ye : 2 * ye], p_send.at[1], p_recv.at[1], down_y),
        send(
            press.at[cells - ze : cells], halo_p.at[2 * ye : 2 * ye + ze],
            p_send.at[2], p_recv.at[2], up_z,
        ),
        send(
            press.at[0:ze], halo_p.at[2 * ye + ze : 2 * ye + 2 * ze],
            p_send.at[3], p_recv.at[3], down_z,
        ),
    ]
    grad[0] = dot(own[...], p[0]) + dot(own[...], p[1]) + dot(own[...], p[2])
    grad_x[0] = dot(p[0], along_x[...]) + dot(p[1], along_x[...]) + dot(p[2], along_x[...])
    for copy in halo_copies:
        copy.wait()
    h = split(halo_p[...], 3)
    grad[0] += dot(beside[...], h[0]) + dot(beside[...], h[1]) + dot(beside[...], h[2])

    def project(i, carry):
        rows = pl.ds(pl.multiple_of(i * 16, 16), 16)
        rows_z = pl.ds(pl.multiple_of(cells + i * 16, 16), 16)
        push = [
            grad_x[0, rows, :] * sixtieth, grad[0, rows, :] * sixtieth, grad[0, rows_z, :] * sixtieth
        ]
        for c in range(3):
            motion[c, rows, :] = prov[c, rows, :] - (
                metric[c, 0] * push[0] + metric[c, 1] * push[1] + metric[c, 2] * push[2]
            )
        return carry

    lax.fori_loop(0, cells // 16, project, 0)


def shards(flow_state, metric, deformation):
    gy, gz = lax.axis_size("gy"), lax.axis_size("gz")
    owners = gy * gz
    _, ez, ey, lx = flow_state.shape
    cells = ez * ey
    m = lx // 2 // owners
    own, beside, pick, along_x = stencil_tables(ez, ey, lx)
    cos_x, sin_x, weight = x_tables(lx)
    ahead = by_owner(cos_x, sin_x, owners)
    back = by_owner(cos_x * weight, sin_x * weight, owners)
    twist, kron, block, ky, kz, edge = plane_tables(gy, gz, ey, ez)
    eye = np.eye(m)
    br, bi = np.cos(block), np.sin(block)
    pair = np.stack([np.stack([br, -bi], 1), np.stack([bi, br], 1)], 0)
    across = np.einsum("atsb,mn->atmsbn", pair.transpose(0, 1, 3, 2), eye)
    across = across.reshape(lx, lx)
    wr, wi = np.cos(kron), np.sin(kron)
    within = np.block([[wr, wi], [-wi, wr]])
    big = np.stack(
        halves(ahead) + halves(back) + halves(across) + halves(across.T)
        + halves(within) + halves(within.T)
    )
    plane = np.repeat(
        np.stack([np.cos(twist), np.sin(twist), ky, kz, edge.astype(np.float64)]), m, axis=1
    ).astype(np.float32)
    bf = jnp.bfloat16
    f32 = jnp.float32
    vmem = pl.BlockSpec(memory_space=pltpu.VMEM)
    smem = pl.BlockSpec(memory_space=pltpu.SMEM)
    hbm = pl.BlockSpec(memory_space=pl.ANY)
    wide = 6 * ez + 8 * ey
    dma = pltpu.SemaphoreType.DMA
    motion, heat_next = pl.pallas_call(
        lambda *refs: kernel((gy, gz, ez, ey, lx), *refs),
        out_shape=(
            jax.ShapeDtypeStruct((3, cells, lx), f32), jax.ShapeDtypeStruct((cells, lx), f32)
        ),
        in_specs=[smem, smem] + [vmem] * 6 + [hbm] * 2,
        out_specs=(vmem, vmem),
        scratch_shapes=[
            pltpu.VMEM(big.shape, bf),
            pltpu.VMEM(plane.shape, f32),
            pltpu.VMEM((2, 4, 3 * ez, lx), bf),
            pltpu.VMEM((4, wide, lx), bf),
            pltpu.VMEM((4, 2 * cells, lx), f32),
            pltpu.VMEM((4, cells, lx), f32),
            pltpu.VMEM((3, cells, lx), f32),
            pltpu.VMEM((3, cells, lx), f32),
            pltpu.VMEM((6 * ez, lx), f32),
            pltpu.VMEM((wide, lx), f32),
            pltpu.VMEM((cells, lx), f32),
            pltpu.VMEM((6 * ez, lx), f32),
            pltpu.VMEM((wide, lx), f32),
            pltpu.VMEM((cells, lx), f32),
            pltpu.VMEM((lx, cells), f32),
        ]
        + [pltpu.VMEM((owners, 2 * m, cells), f32)] * 4
        + [pltpu.VMEM((lx // 2, cells), f32)]
        + [dma((2,))] + [dma((4,))] * 6 + [dma((owners,))] * 4,
        compiler_params=pltpu.CompilerParams(
            collective_id=0, has_side_effects=True, vmem_limit_bytes=56 * 2**20
        ),
        cost_estimate=pl.CostEstimate(
            flops=4 * 10**9, bytes_accessed=12 * 2**20, transcendentals=0
        ),
        name="substep",
    )(
        metric, deformation, flow_state.reshape(4, cells, lx),
        jnp.asarray(own, bf), jnp.asarray(beside, bf),
        jnp.asarray(beside[:cells] + beside[cells:], bf), jnp.asarray(pick, bf),
        jnp.asarray(along_x, bf), jnp.asarray(big), jnp.asarray(plane),
    )
    return motion.reshape(3, ez, ey, lx), heat_next.reshape(ez, ey, lx)

def solution(mesh):
    placed = (P(None, "gz", "gy", None), P(), P())
    return jax.shard_map(
        shards,
        mesh=mesh,
        in_specs=placed,
        out_specs=(P(None, "gz", "gy", None), P("gz", "gy", None)),
        check_vma=False,
    )
```

time: 153 us -> 88.6 us (0.58)
  the two profiles are of different devices: /device:TPU:0 before, /device:TPU:2 now
where the time goes in v1:
time: 88.6 us; the launch traced here: 88.5 us
  Pallas kernels  84.3 us (95%)
  local copies, waits for them, and re-layouts  3.52 us (4%)
    pallas_call x1, Pallas kernels, shards(): pl.pallas_call(lambda *refs: kernel((gy, gz, ez, ey, lx), *refs), out_sha...  84.3 us
    unnamed x4, local copies, waits for them, and re-layouts  3.52 us

profile of v1, /device:TPU:2, one launch (start us, length us, event | category | flops | bytes accessed | tf_op | source)
XLA Modules:
  0.0 88.5 jit_solution(6058263678130231154)
XLA Ops:
  0.6 84.3 %substep.1 = (f32[3,256,512]{2,1,0:T(8,128)}, f32[256,512]{1,0:T(8,128)}) custom-call(f32[3,3]{1,0:T(4,128)} %refs_0_.1, f32[3,3]{1,0:T(4,128)} %refs_1_.1, bf16[4,256,512]{2,1,0:T(8,128)(2,1)} %bitcast.5, bf16[512,256]{1,0:T(8,128)(2,1)} %constant.14.clone.refs_3_, bf16[512,256]{1,0:T(8,128)(2,1)} %constant.15.clone.refs_4_, ...), custom_call_target="tpu_custom_call" | custom-call | flops 4000000000 | bytes 12582912 | tf_op jit(solution)/shard_map/substep/pallas_call | solution.py:393
  84.9 0.0 copy-start
  84.9 2.7 %copy.14 = f32[3,32,8,512]{3,2,1,0:T(8,128)} copy(f32[3,32,8,512]{3,2,1,0:T(8,128)} %bitcast.3) | data formatting | bytes 3145728
  87.7 0.0 copy-done
  87.7 0.8 copy.15
Async XLA Ops:
  84.9 2.7 %copy-start = (f32[256,512]{1,0:T(8,128)S(1)}, f32[256,512]{1,0:T(8,128)}, u32[]{:S(2)}) copy-start(f32[256,512]{1,0:T(8,128)} %get-tuple-element.5) | copy-start | bytes 1572868

commit v2 on v1

--- a/solution.py
+++ b/solution.py
@@ -8,6 +8,7 @@
 from jax.sharding import PartitionSpec as P
 
 substep_width = 0.4
+parts = 2
 mesh_ids = pl.DeviceIdType.MESH
 coefs = {1: 45.0, 2: -9.0, 3: 1.0, -1: -45.0, -2: 9.0, -3: -1.0}
 
@@ -55,31 +56,33 @@
 
 
 def stencil_tables(ez, ey, lx):
-    cells = ez * ey
+    cells, zc = ez * ey, ez // parts
+    part = zc * ey
     own = np.zeros((2 * cells, cells))
-    beside = np.zeros((2 * cells, 6 * ez + 8 * ey))
-    pick = np.zeros((6 * ez, cells))
+    beside = np.zeros((parts, 2 * part, 6 * zc + 4 * ey))
+    pick = np.zeros((6 * zc, part))
     for z in range(ez):
+        h, zh = z // zc, z % zc
         for y in range(ey):
-            r = z * ey + y
+            r, rh = z * ey + y, zh * ey + y
             for o, w in coefs.items():
                 t = y + o
                 if 0 <= t < ey:
                     own[r, z * ey + t] += w
                 elif t < 0:
-                    beside[r, (t + 3) * ez + z] += w
+                    beside[h, rh, (t + 3) * zc + zh] += w
                 else:
-                    beside[r, (3 + t - ey) * ez + z] += w
+                    beside[h, rh, (3 + t - ey) * zc + zh] += w
                 t = z + o
                 if 0 <= t < ez:
                     own[cells + r, t * ey + y] += w
                 elif t < 0:
-                    beside[cells + r, 6 * ez + (t + 4) * ey + y] += w
+                    beside[h, part + rh, 6 * zc + (t + 4) * ey + y] += w
                 else:
-                    beside[cells + r, 6 * ez + 4 * ey + (t - ez) * ey + y] += w
+                    beside[h, part + rh, 6 * zc + (t - ez) * ey + y] += w
         for j in range(3):
-            pick[j * ez + z, z * ey + ey - 3 + j] = 1.0
-            pick[(3 + j) * ez + z, z * ey + j] = 1.0
+            pick[j * zc + zh, zh * ey + ey - 3 + j] = 1.0
+            pick[(3 + j) * zc + zh, zh * ey + j] = 1.0
     along_x = np.zeros((lx, lx))
     for o, w in coefs.items():
         x = np.arange(lx)
@@ -122,7 +125,10 @@
     cells = ez * ey
     rows2 = lx // owners
     m = rows2 // 2
-    ye, ze = 3 * ez, 4 * ey
+    zc = ez // parts
+    part = zc * ey
+    ye, ze = 3 * zc, 4 * ey
+    last = parts - 1
     iy, iz = lax.axis_index("gy"), lax.axis_index("gz")
     me = iy * gz + iz
     up_y = (lax.rem(iy + 1, gy), iz)
@@ -146,10 +152,11 @@
 
     lax.fori_loop(1, owners, greet, 0)
 
-    for c in range(4):
-        picked = dot(pick[...], state[c]).astype(jnp.bfloat16)
-        edge_state[0, c] = picked[:ye]
-        edge_state[1, c] = picked[ye:]
+    for h in range(parts):
+        for c in range(4):
+            picked = dot(pick[...], state[c, h * part : (h + 1) * part]).astype(jnp.bfloat16)
+            edge_state[h, 0, c] = picked[:ye]
+            edge_state[h, 1, c] = picked[ye:]
     pl.semaphore_wait(barrier, owners - 1)
 
     def send(src, dst, send_sem, recv_sem, to):
@@ -160,25 +167,53 @@
         copy.start()
         return copy
 
-    halo_copies = [
-        send(edge_state.at[0], halo_state.at[:, 0:ye], s_send.at[0], s_recv.at[0], up_y),
-        send(edge_state.at[1], halo_state.at[:, ye : 2 * ye], s_send.at[1], s_recv.at[1], down_y),
+    side_z = [
         send(
-            state.at[:, cells - ze : cells], halo_state.at[:, 2 * ye : 2 * ye + ze],
-            s_send.at[2], s_recv.at[2], up_z,
+            state.at[:, cells - ze : cells], halo_state.at[0, :, 2 * ye : 2 * ye + ze],
+            s_send.at[2 * parts], s_recv.at[2 * parts], up_z,
         ),
         send(
-            state.at[:, 0:ze], halo_state.at[:, 2 * ye + ze : 2 * ye + 2 * ze],
-            s_send.at[3], s_recv.at[3], down_z,
+            state.at[:, 0:ze], halo_state.at[last, :, 2 * ye : 2 * ye + ze],
+            s_send.at[2 * parts + 1], s_recv.at[2 * parts + 1], down_z,
         ),
+    ]
+    side_y = [
+        [
+            send(
+                edge_state.at[h, w], halo_state.at[h, :, w * ye : (w + 1) * ye],
+                s_send.at[2 * h + w], s_recv.at[2 * h + w], (up_y, down_y)[w],
+            )
+            for w in range(2)
+        ]
+        for h in range(parts)
     ]
     for c in range(4):
         grad[c] = dot(own[...], state[c])
         grad_x[c] = dot(state[c], along_x[...])
-    for copy in halo_copies:
-        copy.wait()
-    for c in range(4):
-        grad[c] += dot(beside[...], halo_state[c])
+
+    def borders(field, edges, halo, sends, recvs):
+        def side(h):
+            return [
+                send(
+                    edges.at[h, w * ye : (w + 1) * ye], halo.at[h, w * ye : (w + 1) * ye],
+                    sends.at[2 * h + w], recvs.at[2 * h + w], (up_y, down_y)[w],
+                )
+                for w in range(2)
+            ]
+
+        def low():
+            return send(
+                field.at[0:ze], halo.at[last, 2 * ye : 2 * ye + ze],
+                sends.at[2 * parts + 1], recvs.at[2 * parts + 1], down_z,
+            )
+
+        def top():
+            return send(
+                field.at[cells - ze : cells], halo.at[0, 2 * ye : 2 * ye + ze],
+                sends.at[2 * parts], recvs.at[2 * parts], up_z,
+            )
+
+        return side, low, top
 
     sixtieth = 1.0 / 60.0
 
@@ -210,24 +245,30 @@
             flux[j, rows, :] = metric[0, j] * new[0] + metric[1, j] * new[1] + metric[2, j] * new[2]
         return carry
 
-    lax.fori_loop(0, cells // 16, advance, 0)
-
+    side_f, low_f, top_f = borders(flux.at[2], edge_f, halo_f, f_send, f_recv)
+    f_side = []
+    for h in range(parts):
+        for copy in side_y[h]:
+            copy.wait()
+        if h == 0:
+            for copy in side_z:
+                copy.wait()
+        lo, hi = h * part, (h + 1) * part
+        for c in range(4):
+            more = dot(beside[h], halo_state[h, c])
+            grad[c, lo:hi] += more[:part]
+            grad[c, cells + lo : cells + hi] += more[part:]
+        lax.fori_loop(lo // 16, hi // 16, advance, 0)
+        f1 = split(flux[1, lo:hi])
+        edge_f[h] = dot(pick[...], f1[0]) + dot(pick[...], f1[1])
+        f_side.append(side_f(h))
+        if h == 0:
+            f_low = low_f()
+    f_top = top_f()
+
+    f0 = split(flux[0])
     f1 = split(flux[1])
     f2 = split(flux[2])
-    edge_f[...] = dot(pick[...], f1[0]) + dot(pick[...], f1[1])
-    halo_copies = [
-        send(edge_f.at[0:ye], halo_f.at[0:ye], f_send.at[0], f_recv.at[0], up_y),
-        send(edge_f.at[ye : 2 * ye], halo_f.at[ye : 2 * ye], f_send.at[1], f_recv.at[1], down_y),
-        send(
-            flux.at[2, cells - ze : cells], halo_f.at[2 * ye : 2 * ye + ze],
-            f_send.at[2], f_recv.at[2], up_z,
-        ),
-        send(
-            flux.at[2, 0:ze], halo_f.at[2 * ye + ze : 2 * ye + 2 * ze],
-            f_send.at[3], f_recv.at[3], down_z,
-        ),
-    ]
-    f0 = split(flux[0])
     div[...] = (
         dot(f0[0], along_x[...]) + dot(f0[1], along_x[...])
         + dot(own[0:cells], f1[0]) + dot(own[0:cells], f1[1])
@@ -235,31 +276,29 @@
     )
     load_big.wait()
     load_plane.wait()
-    for copy in halo_copies:
-        copy.wait()
-    h = split(halo_f[...])
-    d = split((div[...] + dot(beside_sum[...], h[0]) + dot(beside_sum[...], h[1])) * sixtieth)
-
-    def spread(buffer):
+
+    def spread(buffer, lo, hi):
         if rows2 % 8 == 0:
-            buffer[...] = line[...].reshape(owners, rows2, cells)
+            buffer[:, :, lo:hi] = line[:, lo:hi].reshape(owners, rows2, hi - lo)
         else:
             for k in range(owners):
-                buffer[k] = line[k * rows2 : (k + 1) * rows2, :]
-
-    def gather(buffer):
+                buffer[k, :, lo:hi] = line[k * rows2 : (k + 1) * rows2, lo:hi]
+
+    def gather(buffer, lo, hi):
         if rows2 % 8 == 0:
-            return buffer[...].reshape(owners * rows2, cells)
+            return buffer[:, :, lo:hi].reshape(owners * rows2, hi - lo)
         for k in range(owners):
-            line[k * rows2 : (k + 1) * rows2, :] = buffer[k]
-        return line[...]
-
-    def exchange(source, target, send_sem, recv_sem, meanwhile):
+            line[k * rows2 : (k + 1) * rows2, lo:hi] = buffer[k, :, lo:hi]
+        return line[:, lo:hi]
+
+    def exchange(source, target, send_sem, recv_sem, h):
+        lanes = slice(h * part, (h + 1) * part)
+
         def copy_of(i):
             other = lax.rem(me + i, owners)
             return pltpu.make_async_remote_copy(
-                src_ref=source.at[other], dst_ref=target.at[me],
-                send_sem=send_sem.at[i], recv_sem=recv_sem.at[i],
+                src_ref=source.at[other, :, lanes], dst_ref=target.at[me, :, lanes],
+                send_sem=send_sem.at[h, i], recv_sem=recv_sem.at[h, i],
                 device_id=(other // gz, lax.rem(other, gz)), device_id_type=mesh_ids,
             )
 
@@ -272,9 +311,8 @@
             return carry
 
         lax.fori_loop(1, owners, begin, 0)
-        target[me] = source[me]
-        meanwhile()
-        lax.fori_loop(1, owners, end, 0)
+        target[me, :, lanes] = source[me, :, lanes]
+        return lambda: lax.fori_loop(1, owners, end, 0)
 
     def make_factor():
         row = lax.broadcasted_iota(jnp.int32, (2 * m * owners // 2, cells), 0)
@@ -302,12 +340,26 @@
         total = float(lx * ey * gy * ez * gz)
         factor[...] = jnp.where(at_edge, 0.0, -1.0 / (jnp.where(at_edge, 1.0, symbol) * total))
 
-    line[...] = dot3((big[0], big[1]), d, 1, 1)
-    spread(there)
-    exchange(there, here, a_send, a_recv, make_factor)
+    pending = []
+    for h in range(parts):
+        for copy in f_side[h]:
+            copy.wait()
+        if h == 0:
+            f_top.wait()
+        if h == last:
+            f_low.wait()
+        lo, hi = h * part, (h + 1) * part
+        e = split(halo_f[h])
+        d = split((div[lo:hi] + dot(beside_sum[h], e[0]) + dot(beside_sum[h], e[1])) * sixtieth)
+        line[:, lo:hi] = dot3((big[0], big[1]), d, 1, 1)
+        spread(there, lo, hi)
+        pending.append(exchange(there, here, a_send, a_recv, h))
+    make_factor()
+    for done in pending:
+        done()
 
     half = lx // 2
-    out = dot3((big[4], big[5]), split(gather(here)))
+    out = dot3((big[4], big[5]), split(gather(here, 0, cells)))
     re, im = out[:half], out[half:]
     tr, ti = plane[0], plane[1]
     both = jnp.concatenate([re * tr - im * ti, re * ti + im * tr], axis=1)
@@ -318,30 +370,37 @@
     re, im = out[:, :cells], out[:, cells:]
     both = jnp.concatenate([re * tr + im * ti, im * tr - re * ti], axis=0)
     line[...] = dot3((big[6], big[7]), split(both))
-    spread(there2)
-    exchange(there2, here2, b_send, b_recv, lambda: None)
-
-    press[...] = dot3(split(gather(here2)), (big[2], big[3]), 0, 0)
+    pending = []
+    for h in range(parts):
+        spread(there2, h * part, (h + 1) * part)
+        pending.append(exchange(there2, here2, b_send, b_recv, h))
+    side_p, low_p, top_p = borders(press, edge_p, halo_p, p_send, p_recv)
+    p_side = []
+    for h in range(parts):
+        pending[h]()
+        lo, hi = h * part, (h + 1) * part
+        press[lo:hi] = dot3(split(gather(here2, lo, hi)), (big[2], big[3]), 0, 0)
+        p = split(press[lo:hi], 3)
+        edge_p[h] = dot(pick[...], p[0]) + dot(pick[...], p[1]) + dot(pick[...], p[2])
+        p_side.append(side_p(h))
+        if h == 0:
+            p_low = low_p()
+    p_top = top_p()
     p = split(press[...], 3)
-    edge_p[...] = dot(pick[...], p[0]) + dot(pick[...], p[1]) + dot(pick[...], p[2])
-    halo_copies = [
-        send(edge_p.at[0:ye], halo_p.at[0:ye], p_send.at[0], p_recv.at[0], up_y),
-        send(edge_p.at[ye : 2 * ye], halo_p.at[ye : 2 * ye], p_send.at[1], p_recv.at[1], down_y),
-        send(
-            press.at[cells - ze : cells], halo_p.at[2 * ye : 2 * ye + ze],
-            p_send.at[2], p_recv.at[2], up_z,
-        ),
-        send(
-            press.at[0:ze], halo_p.at[2 * ye + ze : 2 * ye + 2 * ze],
-            p_send.at[3], p_recv.at[3], down_z,
-        ),
-    ]
     grad[0] = dot(own[...], p[0]) + dot(own[...], p[1]) + dot(own[...], p[2])
     grad_x[0] = dot(p[0], along_x[...]) + dot(p[1], along_x[...]) + dot(p[2], along_x[...])
-    for copy in halo_copies:
-        copy.wait()
-    h = split(halo_p[...], 3)
-    grad[0] += dot(beside[...], h[0]) + dot(beside[...], h[1]) + dot(beside[...], h[2])
+    for h in range(parts):
+        for copy in p_side[h]:
+            copy.wait()
+        if h == 0:
+            p_top.wait()
+        if h == last:
+            p_low.wait()
+        lo, hi = h * part, (h + 1) * part
+        e = split(halo_p[h], 3)
+        more = dot(beside[h], e[0]) + dot(beside[h], e[1]) + dot(beside[h], e[2])
+        grad[0, lo:hi] += more[:part]
+        grad[0, cells + lo : cells + hi] += more[part:]
 
     def project(i, carry):
         rows = pl.ds(pl.multiple_of(i * 16, 16), 16)
@@ -388,7 +447,9 @@
     vmem = pl.BlockSpec(memory_space=pltpu.VMEM)
     smem = pl.BlockSpec(memory_space=pltpu.SMEM)
     hbm = pl.BlockSpec(memory_space=pl.ANY)
-    wide = 6 * ez + 8 * ey
+    zc = ez // parts
+    wide = 6 * zc + 4 * ey
+    part = zc * ey
     dma = pltpu.SemaphoreType.DMA
     motion, heat_next = pl.pallas_call(
         lambda *refs: kernel((gy, gz, ez, ey, lx), *refs),
@@ -400,23 +461,23 @@
         scratch_shapes=[
             pltpu.VMEM(big.shape, bf),
             pltpu.VMEM(plane.shape, f32),
-            pltpu.VMEM((2, 4, 3 * ez, lx), bf),
-            pltpu.VMEM((4, wide, lx), bf),
+            pltpu.VMEM((parts, 2, 4, 3 * zc, lx), bf),
+            pltpu.VMEM((parts, 4, wide, lx), bf),
             pltpu.VMEM((4, 2 * cells, lx), f32),
             pltpu.VMEM((4, cells, lx), f32),
             pltpu.VMEM((3, cells, lx), f32),
             pltpu.VMEM((3, cells, lx), f32),
-            pltpu.VMEM((6 * ez, lx), f32),
-            pltpu.VMEM((wide, lx), f32),
+            pltpu.VMEM((parts, 6 * zc, lx), f32),
+            pltpu.VMEM((parts, wide, lx), f32),
             pltpu.VMEM((cells, lx), f32),
-            pltpu.VMEM((6 * ez, lx), f32),
-            pltpu.VMEM((wide, lx), f32),
+            pltpu.VMEM((parts, 6 * zc, lx), f32),
+            pltpu.VMEM((parts, wide, lx), f32),
             pltpu.VMEM((cells, lx), f32),
             pltpu.VMEM((lx, cells), f32),
         ]
         + [pltpu.VMEM((owners, 2 * m, cells), f32)] * 4
         + [pltpu.VMEM((lx // 2, cells), f32)]
-        + [dma((2,))] + [dma((4,))] * 6 + [dma((owners,))] * 4,
+        + [dma((2,))] + [dma((2 * parts + 2,))] * 6 + [dma((parts, owners))] * 4,
         compiler_params=pltpu.CompilerParams(
             collective_id=0, has_side_effects=True, vmem_limit_bytes=56 * 2**20
         ),
@@ -427,7 +488,7 @@
     )(
         metric, deformation, flow_state.reshape(4, cells, lx),
         jnp.asarray(own, bf), jnp.asarray(beside, bf),
-        jnp.asarray(beside[:cells] + beside[cells:], bf), jnp.asarray(pick, bf),
+        jnp.asarray(beside[:, :part] + beside[:, part:], bf), jnp.asarray(pick, bf),
         jnp.asarray(along_x, bf), jnp.asarray(big), jnp.asarray(plane),
     )
     return motion.reshape(3, ez, ey, lx), heat_next.reshape(ez, ey, lx)

time: 88.6 us -> 81.5 us (0.920)
  the two profiles are of different devices: /device:TPU:2 before, /device:TPU:0 now
where the time goes in v2:
time: 81.5 us; the launch traced here: 81.3 us
  Pallas kernels  77.1 us (95%)
  local copies, waits for them, and re-layouts  3.52 us (4%)
    pallas_call x1, Pallas kernels, shards(): pl.pallas_call(lambda *refs: kernel((gy, gz, ez, ey, lx), *refs), out_sha...  77.1 us
    unnamed x4, local copies, waits for them, and re-layouts  3.52 us

profile of v2, /device:TPU:0, one launch (start us, length us, event | category | flops | bytes accessed | tf_op | source)
XLA Modules:
  0.0 81.3 jit_solution(16507759785254844507)
XLA Ops:
  0.6 77.1 %substep.1 = (f32[3,256,512]{2,1,0:T(8,128)}, f32[256,512]{1,0:T(8,128)}) custom-call(f32[3,3]{1,0:T(4,128)} %refs_0_.1, f32[3,3]{1,0:T(4,128)} %refs_1_.1, bf16[4,256,512]{2,1,0:T(8,128)(2,1)} %bitcast.5, bf16[512,256]{1,0:T(8,128)(2,1)} %constant.14.clone.refs_3_, bf16[2,256,128]{2,1,0:T(8,128)(2,1)} %constant.15.clone.refs_4_, ...), custom_call_target="tpu_custom_call" | custom-call | flops 4000000000 | bytes 12582912 | tf_op jit(solution)/shard_map/substep/pallas_call | solution.py:454
  77.8 0.0 copy-start
  77.8 2.7 %copy.14 = f32[3,32,8,512]{3,2,1,0:T(8,128)} copy(f32[3,32,8,512]{3,2,1,0:T(8,128)} %bitcast.3) | data formatting | bytes 3145728
  80.5 0.0 copy-done
  80.5 0.8 copy.15
Async XLA Ops:
  77.8 2.7 %copy-start = (f32[256,512]{1,0:T(8,128)S(1)}, f32[256,512]{1,0:T(8,128)}, u32[]{:S(2)}) copy-start(f32[256,512]{1,0:T(8,128)} %get-tuple-element.5) | copy-start | bytes 1572868

commit v3 on v2

--- a/solution.py
+++ b/solution.py
@@ -141,16 +141,24 @@
     load_big.start()
     load_plane.start()
 
+    def to_all(begin):
+        for dz in range(1, gz):
+            begin(iy, lax.rem(iz + dz, gz))
+
+        def ring(dy, carry):
+            oy = lax.rem(iy + dy, gy)
+            for dz in range(gz):
+                begin(oy, lax.rem(iz + dz, gz))
+            return carry
+
+        lax.fori_loop(1, gy, ring, 0)
+
     barrier = pltpu.get_barrier_semaphore()
 
-    def greet(i, carry):
-        other = lax.rem(me + i, owners)
-        pl.semaphore_signal(
-            barrier, inc=1, device_id=(other // gz, lax.rem(other, gz)), device_id_type=mesh_ids
-        )
-        return carry
-
-    lax.fori_loop(1, owners, greet, 0)
+    def greet(oy, oz):
+        pl.semaphore_signal(barrier, inc=1, device_id=(oy, oz), device_id_type=mesh_ids)
+
+    to_all(greet)
 
     for h in range(parts):
         for c in range(4):
@@ -277,42 +285,39 @@
     load_big.wait()
     load_plane.wait()
 
-    def spread(buffer, lo, hi):
+    def spread(buffer, h):
+        lanes = slice(h * part, (h + 1) * part)
         if rows2 % 8 == 0:
-            buffer[:, :, lo:hi] = line[:, lo:hi].reshape(owners, rows2, hi - lo)
+            buffer[h] = line[:, lanes].reshape(owners, rows2, part)
         else:
             for k in range(owners):
-                buffer[k, :, lo:hi] = line[k * rows2 : (k + 1) * rows2, lo:hi]
-
-    def gather(buffer, lo, hi):
+                buffer[h, k] = line[k * rows2 : (k + 1) * rows2, lanes]
+
+    def gather(buffer, h):
         if rows2 % 8 == 0:
-            return buffer[:, :, lo:hi].reshape(owners * rows2, hi - lo)
+            return buffer[h].reshape(owners * rows2, part)
+        lanes = slice(h * part, (h + 1) * part)
         for k in range(owners):
-            line[k * rows2 : (k + 1) * rows2, lo:hi] = buffer[k, :, lo:hi]
-        return line[:, lo:hi]
+            line[k * rows2 : (k + 1) * rows2, lanes] = buffer[h, k]
+        return line[:, lanes]
 
     def exchange(source, target, send_sem, recv_sem, h):
-        lanes = slice(h * part, (h + 1) * part)
-
-        def copy_of(i):
-            other = lax.rem(me + i, owners)
-            return pltpu.make_async_remote_copy(
-                src_ref=source.at[other, :, lanes], dst_ref=target.at[me, :, lanes],
-                send_sem=send_sem.at[h, i], recv_sem=recv_sem.at[h, i],
-                device_id=(other // gz, lax.rem(other, gz)), device_id_type=mesh_ids,
-            )
-
-        def begin(i, carry):
-            copy_of(i).start()
-            return carry
-
-        def end(i, carry):
-            copy_of(i).wait()
-            return carry
-
-        lax.fori_loop(1, owners, begin, 0)
-        target[me, :, lanes] = source[me, :, lanes]
-        return lambda: lax.fori_loop(1, owners, end, 0)
+        def begin(oy, oz):
+            pltpu.make_async_remote_copy(
+                src_ref=source.at[h, oy * gz + oz], dst_ref=target.at[h, me],
+                send_sem=send_sem.at[h], recv_sem=recv_sem.at[h],
+                device_id=(oy, oz), device_id_type=mesh_ids,
+            ).start()
+
+        to_all(begin)
+        target[h, me] = source[h, me]
+
+        def done():
+            sent, got = source.at[h, 1:owners], target.at[h, 1:owners]
+            pltpu.make_async_copy(got, got, recv_sem.at[h]).wait()
+            pltpu.make_async_copy(sent, sent, send_sem.at[h]).wait()
+
+        return done
 
     def make_factor():
         row = lax.broadcasted_iota(jnp.int32, (2 * m * owners // 2, cells), 0)
@@ -352,14 +357,14 @@
         e = split(halo_f[h])
         d = split((div[lo:hi] + dot(beside_sum[h], e[0]) + dot(beside_sum[h], e[1])) * sixtieth)
         line[:, lo:hi] = dot3((big[0], big[1]), d, 1, 1)
-        spread(there, lo, hi)
+        spread(there, h)
         pending.append(exchange(there, here, a_send, a_recv, h))
     make_factor()
     for done in pending:
         done()
 
     half = lx // 2
-    out = dot3((big[4], big[5]), split(gather(here, 0, cells)))
+    out = dot3((big[4], big[5]), split(jnp.concatenate([gather(here, h) for h in range(parts)], axis=1)))
     re, im = out[:half], out[half:]
     tr, ti = plane[0], plane[1]
     both = jnp.concatenate([re * tr - im * ti, re * ti + im * tr], axis=1)
@@ -372,14 +377,14 @@
     line[...] = dot3((big[6], big[7]), split(both))
     pending = []
     for h in range(parts):
-        spread(there2, h * part, (h + 1) * part)
+        spread(there2, h)
         pending.append(exchange(there2, here2, b_send, b_recv, h))
     side_p, low_p, top_p = borders(press, edge_p, halo_p, p_send, p_recv)
     p_side = []
     for h in range(parts):
         pending[h]()
         lo, hi = h * part, (h + 1) * part
-        press[lo:hi] = dot3(split(gather(here2, lo, hi)), (big[2], big[3]), 0, 0)
+        press[lo:hi] = dot3(split(gather(here2, h)), (big[2], big[3]), 0, 0)
         p = split(press[lo:hi], 3)
         edge_p[h] = dot(pick[...], p[0]) + dot(pick[...], p[1]) + dot(pick[...], p[2])
         p_side.append(side_p(h))
@@ -475,9 +480,9 @@
             pltpu.VMEM((cells, lx), f32),
             pltpu.VMEM((lx, cells), f32),
         ]
-        + [pltpu.VMEM((owners, 2 * m, cells), f32)] * 4
+        + [pltpu.VMEM((parts, owners, 2 * m, part), f32)] * 4
         + [pltpu.VMEM((lx // 2, cells), f32)]
-        + [dma((2,))] + [dma((2 * parts + 2,))] * 6 + [dma((parts, owners))] * 4,
+        + [dma((2,))] + [dma((2 * parts + 2,))] * 6 + [dma((parts,))] * 4,
         compiler_params=pltpu.CompilerParams(
             collective_id=0, has_side_effects=True, vmem_limit_bytes=56 * 2**20
         ),

time: 81.5 us -> 78.6 us (0.964)
  Pallas kernels: 77.1 us -> 74.3 us
    pallas_call x1, Pallas kernels: 77.1 us -> 74.3 us  [shards(): pl.pallas_call(lambda *refs: kernel((gy, gz, ez, ey, lx), *refs), out_sha...]
where the time goes in v3:
time: 78.6 us; the launch traced here: 78.4 us
  Pallas kernels  74.3 us (95%)
  local copies, waits for them, and re-layouts  3.52 us (4%)
    pallas_call x1, Pallas kernels, shards(): pl.pallas_call(lambda *refs: kernel((gy, gz, ez, ey, lx), *refs), out_sha...  74.3 us
    unnamed x4, local copies, waits for them, and re-layouts  3.52 us

profile of v3, /device:TPU:0, one launch (start us, length us, event | category | flops | bytes accessed | tf_op | source)
XLA Modules:
  0.0 78.4 jit_solution(9525683346048884702)
XLA Ops:
  0.6 74.3 %substep.1 = (f32[3,256,512]{2,1,0:T(8,128)}, f32[256,512]{1,0:T(8,128)}) custom-call(f32[3,3]{1,0:T(4,128)} %refs_0_.1, f32[3,3]{1,0:T(4,128)} %refs_1_.1, bf16[4,256,512]{2,1,0:T(8,128)(2,1)} %bitcast.5, bf16[512,256]{1,0:T(8,128)(2,1)} %constant.14.clone.refs_3_, bf16[2,256,128]{2,1,0:T(8,128)(2,1)} %constant.15.clone.refs_4_, ...), custom_call_target="tpu_custom_call" | custom-call | flops 4000000000 | bytes 12582912 | tf_op jit(solution)/shard_map/substep/pallas_call | solution.py:459
  74.9 0.0 copy-start
  74.9 2.7 %copy.14 = f32[3,32,8,512]{3,2,1,0:T(8,128)} copy(f32[3,32,8,512]{3,2,1,0:T(8,128)} %bitcast.3) | data formatting | bytes 3145728
  77.6 0.0 copy-done
  77.6 0.8 %copy.15 = f32[32,8,512]{2,1,0:T(8,128)} copy(f32[32,8,512]{2,1,0:T(8,128)S(1)} %bitcast.4) | data formatting | bytes 1048576
Async XLA Ops:
  74.9 2.7 %copy-start = (f32[256,512]{1,0:T(8,128)S(1)}, f32[256,512]{1,0:T(8,128)}, u32[]{:S(2)}) copy-start(f32[256,512]{1,0:T(8,128)} %get-tuple-element.5) | copy-start | bytes 1572868

commit v4 on v3

--- a/solution.py
+++ b/solution.py
@@ -105,6 +105,25 @@
     return out
 
 
+code_top = 2.0**7.5
+
+
+def encode(x):
+    top = jnp.maximum(jnp.max(jnp.abs(x), axis=0, keepdims=True), 1e-30)
+    t = x * (code_top / top)
+    for _ in range(4):
+        t = t * t
+    return jnp.where(x < 0.0, -t, t), top
+
+
+def decode(code, top):
+    code = code.astype(jnp.float32)
+    size = jnp.abs(code)
+    root = jnp.exp(jnp.log(jnp.maximum(size, 1e-37)) * (1.0 / 16.0)) * (top * (1.0 / code_top))
+    root = jnp.where(size < 1e-37, 0.0, root)
+    return jnp.where(code < 0.0, -root, root)
+
+
 def dot(a, b, ca=1, cb=0):
     return lax.dot_general(a, b, (((ca,), (cb,)), ((), ())), preferred_element_type=jnp.float32)
 
@@ -116,9 +135,9 @@
 def kernel(
     sizes, metric, deform, state, own, beside, beside_sum, pick, along_x, big_hbm, plane_hbm,
     motion, heat_next,
-    big, plane, edge_state, halo_state, grad, grad_x, prov, flux, edge_f, halo_f, div,
+    big, plane, edge_state, halo_state, grad, grad_x, prov, flux, edge_f, halo_f, div, code_f, code_halo_f, top_f, top_halo_f, tops, top_line,
     edge_p, halo_p, press, line, there, here, there2, here2, factor,
-    load_sem, s_send, s_recv, f_send, f_recv, p_send, p_recv, a_send, a_recv, b_send, b_recv,
+    load_sem, t_send, t_recv, u_send, u_recv, s_send, s_recv, f_send, f_recv, p_send, p_recv, a_send, a_recv, b_send, b_recv,
 ):
     gy, gz, ez, ey, lx = sizes
     owners = gy * gz
@@ -200,7 +219,7 @@
         grad_x[c] = dot(state[c], along_x[...])
 
     def borders(field, edges, halo, sends, recvs):
-        def side(h):
+        def side(h, edges=edges, halo=halo):
             return [
                 send(
                     edges.at[h, w * ye : (w + 1) * ye], halo.at[h, w * ye : (w + 1) * ye],
@@ -253,7 +272,7 @@
             flux[j, rows, :] = metric[0, j] * new[0] + metric[1, j] * new[1] + metric[2, j] * new[2]
         return carry
 
-    side_f, low_f, top_f = borders(flux.at[2], edge_f, halo_f, f_send, f_recv)
+    side_f, low_f, high_f = borders(flux.at[2], edge_f, halo_f, f_send, f_recv)
     f_side = []
     for h in range(parts):
         for copy in side_y[h]:
@@ -268,11 +287,22 @@
             grad[c, cells + lo : cells + hi] += more[part:]
         lax.fori_loop(lo // 16, hi // 16, advance, 0)
         f1 = split(flux[1, lo:hi])
-        edge_f[h] = dot(pick[...], f1[0]) + dot(pick[...], f1[1])
-        f_side.append(side_f(h))
+        code, top = encode(dot(pick[...], f1[0]) + dot(pick[...], f1[1]))
+        code_f[h] = code.astype(jnp.bfloat16)
+        top_f[h] = top
+        f_side.append(
+            side_f(h, code_f, code_halo_f)
+            + [
+                send(
+                    top_f.at[h], top_halo_f.at[h, w], t_send.at[2 * h + w], t_recv.at[2 * h + w],
+                    (up_y, down_y)[w],
+                )
+                for w in range(2)
+            ]
+        )
         if h == 0:
             f_low = low_f()
-    f_top = top_f()
+    f_top = high_f()
 
     f0 = split(flux[0])
     f1 = split(flux[1])
@@ -288,36 +318,41 @@
     def spread(buffer, h):
         lanes = slice(h * part, (h + 1) * part)
         if rows2 % 8 == 0:
-            buffer[h] = line[:, lanes].reshape(owners, rows2, part)
+            buffer[h] = line[:, lanes].reshape(owners, rows2, part).astype(buffer.dtype)
         else:
             for k in range(owners):
-                buffer[h, k] = line[k * rows2 : (k + 1) * rows2, lanes]
+                buffer[h, k] = line[k * rows2 : (k + 1) * rows2, lanes].astype(buffer.dtype)
 
     def gather(buffer, h):
         if rows2 % 8 == 0:
-            return buffer[h].reshape(owners * rows2, part)
+            return buffer.reshape(owners * rows2, part)
         lanes = slice(h * part, (h + 1) * part)
         for k in range(owners):
-            line[k * rows2 : (k + 1) * rows2, lanes] = buffer[h, k]
+            line[k * rows2 : (k + 1) * rows2, lanes] = buffer[k]
         return line[:, lanes]
 
-    def exchange(source, target, send_sem, recv_sem, h):
+    def exchange(source, target, send_sem, recv_sem, h, shared=False):
         def begin(oy, oz):
+            src = source.at[h, 0] if shared else source.at[h, oy * gz + oz]
             pltpu.make_async_remote_copy(
-                src_ref=source.at[h, oy * gz + oz], dst_ref=target.at[h, me],
+                src_ref=src, dst_ref=target.at[h, me],
                 send_sem=send_sem.at[h], recv_sem=recv_sem.at[h],
                 device_id=(oy, oz), device_id_type=mesh_ids,
             ).start()
 
         to_all(begin)
-        target[h, me] = source[h, me]
+        target[h, me] = source[h, 0] if shared else source[h, me]
 
         def done():
-            sent, got = source.at[h, 1:owners], target.at[h, 1:owners]
+            got = target.at[h, 1:owners]
+            sent = got if shared else source.at[h, 1:owners]
             pltpu.make_async_copy(got, got, recv_sem.at[h]).wait()
             pltpu.make_async_copy(sent, sent, send_sem.at[h]).wait()
 
         return done
+
+    def share(source, target, send_sem, recv_sem, h):
+        return exchange(source, target, send_sem, recv_sem, h, True)
 
     def make_factor():
         row = lax.broadcasted_iota(jnp.int32, (2 * m * owners // 2, cells), 0)
@@ -354,17 +389,27 @@
         if h == last:
             f_low.wait()
         lo, hi = h * part, (h + 1) * part
+        for w in range(2):
+            rows = slice(w * ye, (w + 1) * ye)
+            halo_f[h, rows] = decode(code_halo_f[h, rows], top_halo_f[h, w])
         e = split(halo_f[h])
         d = split((div[lo:hi] + dot(beside_sum[h], e[0]) + dot(beside_sum[h], e[1])) * sixtieth)
-        line[:, lo:hi] = dot3((big[0], big[1]), d, 1, 1)
+        code, top = encode(dot3((big[0], big[1]), d, 1, 1))
+        line[:, lo:hi] = code
+        top_line[h, 0] = top
         spread(there, h)
         pending.append(exchange(there, here, a_send, a_recv, h))
+        pending.append(share(top_line, tops, u_send, u_recv, h))
     make_factor()
     for done in pending:
         done()
 
+    def received(h):
+        return gather(decode(here[h], tops[h]), h)
+
+
     half = lx // 2
-    out = dot3((big[4], big[5]), split(jnp.concatenate([gather(here, h) for h in range(parts)], axis=1)))
+    out = dot3((big[4], big[5]), split(jnp.concatenate([received(h) for h in range(parts)], axis=1)))
     re, im = out[:half], out[half:]
     tr, ti = plane[0], plane[1]
     both = jnp.concatenate([re * tr - im * ti, re * ti + im * tr], axis=1)
@@ -384,7 +429,7 @@
     for h in range(parts):
         pending[h]()
         lo, hi = h * part, (h + 1) * part
-        press[lo:hi] = dot3(split(gather(here2, h)), (big[2], big[3]), 0, 0)
+        press[lo:hi] = dot3(split(gather(here2[h], h)), (big[2], big[3]), 0, 0)
         p = split(press[lo:hi], 3)
         edge_p[h] = dot(pick[...], p[0]) + dot(pick[...], p[1]) + dot(pick[...], p[2])
         p_side.append(side_p(h))
@@ -475,14 +520,21 @@
             pltpu.VMEM((parts, 6 * zc, lx), f32),
             pltpu.VMEM((parts, wide, lx), f32),
             pltpu.VMEM((cells, lx), f32),
+            pltpu.VMEM((parts, 6 * zc, lx), bf),
+            pltpu.VMEM((parts, 6 * zc, lx), bf),
+            pltpu.VMEM((parts, 1, lx), f32),
+            pltpu.VMEM((parts, 2, 1, lx), f32),
+            pltpu.VMEM((parts, owners, 1, part), f32),
+            pltpu.VMEM((parts, 1, 1, part), f32),
             pltpu.VMEM((parts, 6 * zc, lx), f32),
             pltpu.VMEM((parts, wide, lx), f32),
             pltpu.VMEM((cells, lx), f32),
             pltpu.VMEM((lx, cells), f32),
         ]
-        + [pltpu.VMEM((parts, owners, 2 * m, part), f32)] * 4
+        + [pltpu.VMEM((parts, owners, 2 * m, part), bf)] * 2
+        + [pltpu.VMEM((parts, owners, 2 * m, part), f32)] * 2
         + [pltpu.VMEM((lx // 2, cells), f32)]
-        + [dma((2,))] + [dma((2 * parts + 2,))] * 6 + [dma((parts,))] * 4,
+        + [dma((2,))] + [dma((2 * parts,))] * 2 + [dma((parts,))] * 2 + [dma((2 * parts + 2,))] * 6 + [dma((parts,))] * 4,
         compiler_params=pltpu.CompilerParams(
             collective_id=0, has_side_effects=True, vmem_limit_bytes=56 * 2**20
         ),

time: 78.6 us -> 73.5 us (0.935)
  Pallas kernels: 74.3 us -> 69.1 us
    pallas_call x1, Pallas kernels: 74.3 us -> 69.1 us  [shards(): pl.pallas_call(lambda *refs: kernel((gy, gz, ez, ey, lx), *refs), out_sha...]
where the time goes in v4:
time: 73.5 us; the launch traced here: 73.3 us
  Pallas kernels  69.1 us (94%)
  local copies, waits for them, and re-layouts  3.52 us (5%)
    pallas_call x1, Pallas kernels, shards(): pl.pallas_call(lambda *refs: kernel((gy, gz, ez, ey, lx), *refs), out_sha...  69.1 us
    unnamed x4, local copies, waits for them, and re-layouts  3.52 us

profile of v4, /device:TPU:0, one launch (start us, length us, event | category | flops | bytes accessed | tf_op | source)
XLA Modules:
  0.0 73.3 jit_solution(7321331396587188417)
XLA Ops:
  0.6 69.1 %substep.1 = (f32[3,256,512]{2,1,0:T(8,128)}, f32[256,512]{1,0:T(8,128)}) custom-call(f32[3,3]{1,0:T(4,128)} %refs_0_.1, f32[3,3]{1,0:T(4,128)} %refs_1_.1, bf16[4,256,512]{2,1,0:T(8,128)(2,1)} %bitcast.5, bf16[512,256]{1,0:T(8,128)(2,1)} %constant.14.clone.refs_3_, bf16[2,256,128]{2,1,0:T(8,128)(2,1)} %constant.15.clone.refs_4_, ...), custom_call_target="tpu_custom_call" | custom-call | flops 4000000000 | bytes 12582912 | tf_op jit(solution)/shard_map/substep/pallas_call | solution.py:504
  69.7 0.0 copy-start
  69.8 2.7 %copy.14 = f32[3,32,8,512]{3,2,1,0:T(8,128)} copy(f32[3,32,8,512]{3,2,1,0:T(8,128)} %bitcast.3) | data formatting | bytes 3145728
  72.5 0.0 copy-done
  72.5 0.8 %copy.15 = f32[32,8,512]{2,1,0:T(8,128)} copy(f32[32,8,512]{2,1,0:T(8,128)S(1)} %bitcast.4) | data formatting | bytes 1048576
Async XLA Ops:
  69.7 2.7 %copy-start = (f32[256,512]{1,0:T(8,128)S(1)}, f32[256,512]{1,0:T(8,128)}, u32[]{:S(2)}) copy-start(f32[256,512]{1,0:T(8,128)} %get-tuple-element.5) | copy-start | bytes 1572868

commit v5 on v4

--- a/solution.py
+++ b/solution.py
@@ -204,16 +204,16 @@
             s_send.at[2 * parts + 1], s_recv.at[2 * parts + 1], down_z,
         ),
     ]
-    side_y = [
-        [
+    def side_state(h):
+        return [
             send(
                 edge_state.at[h, w], halo_state.at[h, :, w * ye : (w + 1) * ye],
                 s_send.at[2 * h + w], s_recv.at[2 * h + w], (up_y, down_y)[w],
             )
             for w in range(2)
         ]
-        for h in range(parts)
-    ]
+
+    side_y = [side_state(0)]
     for c in range(4):
         grad[c] = dot(own[...], state[c])
         grad_x[c] = dot(state[c], along_x[...])
@@ -276,7 +276,11 @@
     f_side = []
     for h in range(parts):
         for copy in side_y[h]:
-            copy.wait()
+            copy.wait_send()
+        if h < last:
+            side_y.append(side_state(h + 1))
+        for copy in side_y[h]:
+            copy.wait_recv()
         if h == 0:
             for copy in side_z:
                 copy.wait()

time: 73.5 us -> 74.3 us (1.011)
  Pallas kernels: 69.1 us -> 69.9 us
    pallas_call x1, Pallas kernels: 69.1 us -> 69.9 us  [shards(): pl.pallas_call(lambda *refs: kernel((gy, gz, ez, ey, lx), *refs), out_sha...]
where the time goes in v5:
time: 74.3 us; the launch traced here: 74.1 us
  Pallas kernels  69.9 us (94%)
  local copies, waits for them, and re-layouts  3.52 us (5%)
    pallas_call x1, Pallas kernels, shards(): pl.pallas_call(lambda *refs: kernel((gy, gz, ez, ey, lx), *refs), out_sha...  69.9 us
    unnamed x4, local copies, waits for them, and re-layouts  3.52 us

profile of v5, /device:TPU:0, one launch (start us, length us, event | category | flops | bytes accessed | tf_op | source)
XLA Modules:
  0.0 74.1 jit_solution(12799304145447717318)
XLA Ops:
  0.6 69.9 %substep.1 = (f32[3,256,512]{2,1,0:T(8,128)}, f32[256,512]{1,0:T(8,128)}) custom-call(f32[3,3]{1,0:T(4,128)} %refs_0_.1, f32[3,3]{1,0:T(4,128)} %refs_1_.1, bf16[4,256,512]{2,1,0:T(8,128)(2,1)} %bitcast.5, bf16[512,256]{1,0:T(8,128)(2,1)} %constant.14.clone.refs_3_, bf16[2,256,128]{2,1,0:T(8,128)(2,1)} %constant.15.clone.refs_4_, ...), custom_call_target="tpu_custom_call" | custom-call | flops 4000000000 | bytes 12582912 | tf_op jit(solution)/shard_map/substep/pallas_call | solution.py:508
  70.6 0.0 copy-start
  70.6 2.7 %copy.14 = f32[3,32,8,512]{3,2,1,0:T(8,128)} copy(f32[3,32,8,512]{3,2,1,0:T(8,128)} %bitcast.3) | data formatting | bytes 3145728
  73.3 0.0 copy-done
  73.3 0.8 %copy.15 = f32[32,8,512]{2,1,0:T(8,128)} copy(f32[32,8,512]{2,1,0:T(8,128)S(1)} %bitcast.4) | data formatting | bytes 1048576
Async XLA Ops:
  70.6 2.7 %copy-start = (f32[256,512]{1,0:T(8,128)S(1)}, f32[256,512]{1,0:T(8,128)}, u32[]{:S(2)}) copy-start(f32[256,512]{1,0:T(8,128)} %get-tuple-element.5) | copy-start | bytes 1572868

commit v6 on v4

--- a/solution.py
+++ b/solution.py
@@ -134,10 +134,10 @@
 
 def kernel(
     sizes, metric, deform, state, own, beside, beside_sum, pick, along_x, big_hbm, plane_hbm,
-    motion, heat_next,
-    big, plane, edge_state, halo_state, grad, grad_x, prov, flux, edge_f, halo_f, div, code_f, code_halo_f, top_f, top_halo_f, tops, top_line,
+    prov_out, heat_out, push_x_out, push_yz_out,
+    heat_next, big, plane, edge_state, halo_state, grad, grad_x, prov, flux, edge_f, halo_f, div, code_f, code_halo_f, top_f, top_halo_f, tops, top_line,
     edge_p, halo_p, press, line, there, here, there2, here2, factor,
-    load_sem, t_send, t_recv, u_send, u_recv, s_send, s_recv, f_send, f_recv, p_send, p_recv, a_send, a_recv, b_send, b_recv,
+    load_sem, out_sem, t_send, t_recv, u_send, u_recv, s_send, s_recv, f_send, f_recv, p_send, p_recv, a_send, a_recv, b_send, b_recv,
 ):
     gy, gz, ez, ey, lx = sizes
     owners = gy * gz
@@ -303,6 +303,12 @@
         if h == 0:
             f_low = low_f()
     f_top = high_f()
+    outgoing = [
+        pltpu.make_async_copy(prov, prov_out, out_sem.at[0]),
+        pltpu.make_async_copy(heat_next, heat_out, out_sem.at[1]),
+    ]
+    for copy in outgoing:
+        copy.start()
 
     f0 = split(flux[0])
     f1 = split(flux[1])
@@ -401,15 +407,15 @@
         pending.append(exchange(there, here, a_send, a_recv, h))
         pending.append(share(top_line, tops, u_send, u_recv, h))
     make_factor()
-    for done in pending:
-        done()
-
-    def received(h):
-        return gather(decode(here[h], tops[h]), h)
-
 
     half = lx // 2
-    out = dot3((big[4], big[5]), split(jnp.concatenate([received(h) for h in range(parts)], axis=1)))
+    halved = []
+    for h in range(parts):
+        pending[2 * h]()
+        pending[2 * h + 1]()
+        block = gather(decode(here[h], tops[h]), h)
+        halved.append(dot3((big[4], big[5]), split(block)))
+    out = jnp.concatenate(halved, axis=1)
     re, im = out[:half], out[half:]
     tr, ti = plane[0], plane[1]
     both = jnp.concatenate([re * tr - im * ti, re * ti + im * tr], axis=1)
@@ -419,9 +425,11 @@
     out = dot3(split(both), (big[10], big[11]))
     re, im = out[:, :cells], out[:, cells:]
     both = jnp.concatenate([re * tr + im * ti, im * tr - re * ti], axis=0)
-    line[...] = dot3((big[6], big[7]), split(both))
+    both = split(both)
     pending = []
     for h in range(parts):
+        lanes = slice(h * part, (h + 1) * part)
+        line[:, lanes] = dot3((big[6], big[7]), [b[:, lanes] for b in both])
         spread(there2, h)
         pending.append(exchange(there2, here2, b_send, b_recv, h))
     side_p, low_p, top_p = borders(press, edge_p, halo_p, p_send, p_recv)
@@ -439,6 +447,9 @@
     p = split(press[...], 3)
     grad[0] = dot(own[...], p[0]) + dot(own[...], p[1]) + dot(own[...], p[2])
     grad_x[0] = dot(p[0], along_x[...]) + dot(p[1], along_x[...]) + dot(p[2], along_x[...])
+    copy = pltpu.make_async_copy(grad_x.at[0], push_x_out, out_sem.at[2])
+    copy.start()
+    outgoing.append(copy)
     for h in range(parts):
         for copy in p_side[h]:
             copy.wait()
@@ -451,20 +462,25 @@
         more = dot(beside[h], e[0]) + dot(beside[h], e[1]) + dot(beside[h], e[2])
         grad[0, lo:hi] += more[:part]
         grad[0, cells + lo : cells + hi] += more[part:]
-
-    def project(i, carry):
-        rows = pl.ds(pl.multiple_of(i * 16, 16), 16)
-        rows_z = pl.ds(pl.multiple_of(cells + i * 16, 16), 16)
-        push = [
-            grad_x[0, rows, :] * sixtieth, grad[0, rows, :] * sixtieth, grad[0, rows_z, :] * sixtieth
-        ]
-        for c in range(3):
-            motion[c, rows, :] = prov[c, rows, :] - (
-                metric[c, 0] * push[0] + metric[c, 1] * push[1] + metric[c, 2] * push[2]
+        for k, rows in enumerate((slice(lo, hi), slice(cells + lo, cells + hi))):
+            copy = pltpu.make_async_copy(
+                grad.at[0, rows], push_yz_out.at[rows], out_sem.at[3 + 2 * h + k]
             )
-        return carry
-
-    lax.fori_loop(0, cells // 16, project, 0)
+            copy.start()
+            outgoing.append(copy)
+
+    for copy in outgoing:
+        copy.wait()
+
+
+def project(metric, prov, push_x, push_y, push_z, heat, motion, heat_next):
+    sixtieth = 1.0 / 60.0
+    push = [push_x[...] * sixtieth, push_y[...] * sixtieth, push_z[...] * sixtieth]
+    for c in range(3):
+        motion[c] = prov[c] - (
+            metric[c, 0] * push[0] + metric[c, 1] * push[1] + metric[c, 2] * push[2]
+        )
+    heat_next[...] = heat[...]
 
 
 def shards(flow_state, metric, deformation):
@@ -501,14 +517,16 @@
     wide = 6 * zc + 4 * ey
     part = zc * ey
     dma = pltpu.SemaphoreType.DMA
-    motion, heat_next = pl.pallas_call(
+    prov, heat, push_x, push_yz = pl.pallas_call(
         lambda *refs: kernel((gy, gz, ez, ey, lx), *refs),
         out_shape=(
-            jax.ShapeDtypeStruct((3, cells, lx), f32), jax.ShapeDtypeStruct((cells, lx), f32)
+            jax.ShapeDtypeStruct((3, cells, lx), f32), jax.ShapeDtypeStruct((cells, lx), f32),
+            jax.ShapeDtypeStruct((cells, lx), f32), jax.ShapeDtypeStruct((2 * cells, lx), f32),
         ),
         in_specs=[smem, smem] + [vmem] * 6 + [hbm] * 2,
-        out_specs=(vmem, vmem),
+        out_specs=(hbm,) * 4,
         scratch_shapes=[
+            pltpu.VMEM((cells, lx), f32),
             pltpu.VMEM(big.shape, bf),
             pltpu.VMEM(plane.shape, f32),
             pltpu.VMEM((parts, 2, 4, 3 * zc, lx), bf),
@@ -534,7 +552,7 @@
         + [pltpu.VMEM((parts, owners, 2 * m, part), bf)] * 2
         + [pltpu.VMEM((parts, owners, 2 * m, part), f32)] * 2
         + [pltpu.VMEM((lx // 2, cells), f32)]
-        + [dma((2,))] + [dma((2 * parts,))] * 2 + [dma((parts,))] * 2 + [dma((2 * parts + 2,))] * 6 + [dma((parts,))] * 4,
+        + [dma((2,)), dma((3 + 2 * parts,))] + [dma((2 * parts,))] * 2 + [dma((parts,))] * 2 + [dma((2 * parts + 2,))] * 6 + [dma((parts,))] * 4,
         compiler_params=pltpu.CompilerParams(
             collective_id=0, has_side_effects=True, vmem_limit_bytes=56 * 2**20
         ),
@@ -548,6 +566,23 @@
         jnp.asarray(beside[:, :part] + beside[:, part:], bf), jnp.asarray(pick, bf),
         jnp.asarray(along_x, bf), jnp.asarray(big), jnp.asarray(plane),
     )
+    steps = 4
+    block = cells // steps
+    row = pl.BlockSpec((block, lx), lambda i: (i, 0))
+    motion, heat_next = pl.pallas_call(
+        project,
+        grid=(steps,),
+        out_shape=(
+            jax.ShapeDtypeStruct((3, cells, lx), f32), jax.ShapeDtypeStruct((cells, lx), f32)
+        ),
+        in_specs=[
+            smem, pl.BlockSpec((3, block, lx), lambda i: (0, i, 0)), row, row,
+            pl.BlockSpec((block, lx), lambda i: (i + steps, 0)), row,
+        ],
+        out_specs=(pl.BlockSpec((3, block, lx), lambda i: (0, i, 0)), row),
+        compiler_params=pltpu.CompilerParams(vmem_limit_bytes=32 * 2**20),
+        name="project",
+    )(metric, prov, push_x, push_yz, push_yz, heat)
     return motion.reshape(3, ez, ey, lx), heat_next.reshape(ez, ey, lx)
 
 def solution(mesh):

time: 73.5 us -> 75.9 us (1.033)
  local copies, waits for them, and re-layouts: 3.52 us -> 4.71 us
  Pallas kernels: 69.1 us -> 70.2 us
    pallas_call x0 -> x1, Pallas kernels: none -> 2.65 us  [shards(): pl.pallas_call(project, grid=(steps,), out_shape=(jax.ShapeDtypeStruct((3...]
    pallas_call x1, Pallas kernels: 69.1 us -> 67.6 us  [shards(): pl.pallas_call(lambda *refs: kernel((gy, gz, ez, ey, lx), *refs), out_sha...]
    unnamed x4 -> x10, local copies, waits for them, and re-layouts: 3.52 us -> 4.71 us
where the time goes in v6:
time: 75.9 us; the launch traced here: 75.6 us
  Pallas kernels  70.2 us (92%)
  local copies, waits for them, and re-layouts  4.71 us (6%)
    pallas_call x1, Pallas kernels, shards(): pl.pallas_call(lambda *refs: kernel((gy, gz, ez, ey, lx), *refs), out_sha...  67.6 us
    unnamed x10, local copies, waits for them, and re-layouts  4.71 us
    pallas_call x1, Pallas kernels, shards(): pl.pallas_call(project, grid=(steps,), out_shape=(jax.ShapeDtypeStruct((3...  2.65 us

profile of v6, /device:TPU:0, one launch (start us, length us, event | category | flops | bytes accessed | tf_op | source)
XLA Modules:
  0.0 75.6 jit_solution(15085511605283146969)
XLA Ops:
  0.6 0.0 copy-start.4
  0.6 67.6 %substep.1 = (f32[3,256,512]{2,1,0:T(8,128)}, f32[256,512]{1,0:T(8,128)}, f32[256,512]{1,0:T(8,128)}, f32[512,512]{1,0:T(8,128)}) custom-call(f32[3,3]{1,0:T(4,128)} %metric.1, f32[3,3]{1,0:T(4,128)} %refs_1_.1, bf16[4,256,512]{2,1,0:T(8,128)(2,1)} %bitcast.4, bf16[512,256]{1,0:T(8,128)(2,1)} %constant.14.clone.refs_3_, ...), custom_call_target="tpu_custom_call" | custom-call | flops 4000000000 | bytes 12582912 | tf_op jit(solution)/shard_map/substep/pallas_call | solution.py:520
  68.2 0.0 copy-done.4
  68.2 0.0 copy-start
  68.3 1.2 %copy-done = f32[512,512]{1,0:T(8,128)S(1)} copy-done((f32[512,512]{1,0:T(8,128)S(1)}, f32[512,512]{1,0:T(8,128)}, u32[]{:S(2)}) %copy-start) | copy-done | bytes 1048600
  69.5 0.0 copy-start.1
  69.5 1.4 %copy-done.1 = f32[3,256,512]{2,1,0:T(8,128)S(1)} copy-done((f32[3,256,512]{2,1,0:T(8,128)S(1)}, f32[3,256,512]{2,1,0:T(8,128)}, u32[]{:S(2)}) %copy-start.1) | copy-done | bytes 1572888
  70.9 0.0 copy-start.2
  70.9 1.0 %copy-done.2 = f32[256,512]{1,0:T(8,128)S(1)} copy-done((f32[256,512]{1,0:T(8,128)S(1)}, f32[256,512]{1,0:T(8,128)}, u32[]{:S(2)}) %copy-start.2) | copy-done | bytes 524312
  71.9 0.0 copy-start.3
  71.9 1.0 %copy-done.3 = f32[256,512]{1,0:T(8,128)S(1)} copy-done((f32[256,512]{1,0:T(8,128)S(1)}, f32[256,512]{1,0:T(8,128)}, u32[]{:S(2)}) %copy-start.3) | copy-done | bytes 524312
  73.0 2.6 %project.1 = (f32[3,256,512]{2,1,0:T(8,128)}, f32[256,512]{1,0:T(8,128)}) custom-call(f32[3,3]{1,0:T(4,128)S(1)} %copy-done.4, f32[3,256,512]{2,1,0:T(8,128)S(1)} %copy-done.1, f32[256,512]{1,0:T(8,128)S(1)} %copy-done.3, f32[512,512]{1,0:T(8,128)S(1)} %copy-done, f32[512,512]{1,0:T(8,128)S(1)} %copy-done, f32[256,512]{1,0:T(8,128)S(1)} %copy-done.2), custom_call_target="tpu_custom_call" | custom-call | tf_op jit(solution)/shard_map/project/pallas_call | solution.py:572
Async XLA Ops:
  0.6 67.6 %copy-start.4 = (f32[3,3]{1,0:T(4,128)S(1)}, f32[3,3]{1,0:T(4,128)}, u32[]{:S(2)}) copy-start(f32[3,3]{1,0:T(4,128)} %metric.1) | copy-start | bytes 112
  68.2 1.2 %copy-start = (f32[512,512]{1,0:T(8,128)S(1)}, f32[512,512]{1,0:T(8,128)}, u32[]{:S(2)}) copy-start(f32[512,512]{1,0:T(8,128)} %get-tuple-element.10.push_y.push_z) | copy-start | bytes 3145732
  69.5 1.4 %copy-start.1 = (f32[3,256,512]{2,1,0:T(8,128)S(1)}, f32[3,256,512]{2,1,0:T(8,128)}, u32[]{:S(2)}) copy-start(f32[3,256,512]{2,1,0:T(8,128)} %get-tuple-element.8.prov) | copy-start | bytes 4718596
  70.9 1.0 %copy-start.2 = (f32[256,512]{1,0:T(8,128)S(1)}, f32[256,512]{1,0:T(8,128)}, u32[]{:S(2)}) copy-start(f32[256,512]{1,0:T(8,128)} %get-tuple-element.11.heat) | copy-start | bytes 1572868
  71.9 1.0 %copy-start.3 = (f32[256,512]{1,0:T(8,128)S(1)}, f32[256,512]{1,0:T(8,128)}, u32[]{:S(2)}) copy-start(f32[256,512]{1,0:T(8,128)} %get-tuple-element.9.push_x) | copy-start | bytes 1572868

commit v7 on v6

--- a/solution.py
+++ b/solution.py
@@ -194,6 +194,16 @@
         copy.start()
         return copy
 
+    side_y = [
+        [
+            send(
+                edge_state.at[h, w], halo_state.at[h, :, w * ye : (w + 1) * ye],
+                s_send.at[2 * h + w], s_recv.at[2 * h + w], (up_y, down_y)[w],
+            )
+            for w in range(2)
+        ]
+        for h in range(parts)
+    ]
     side_z = [
         send(
             state.at[:, cells - ze : cells], halo_state.at[0, :, 2 * ye : 2 * ye + ze],
@@ -204,19 +214,39 @@
             s_send.at[2 * parts + 1], s_recv.at[2 * parts + 1], down_z,
         ),
     ]
-    side_y = [
-        [
-            send(
-                edge_state.at[h, w], halo_state.at[h, :, w * ye : (w + 1) * ye],
-                s_send.at[2 * h + w], s_recv.at[2 * h + w], (up_y, down_y)[w],
-            )
-            for w in range(2)
-        ]
-        for h in range(parts)
-    ]
     for c in range(4):
         grad[c] = dot(own[...], state[c])
         grad_x[c] = dot(state[c], along_x[...])
+
+    def make_factor():
+        row = lax.broadcasted_iota(jnp.int32, (2 * m * owners // 2, cells), 0)
+        mode = me * m + (row & (m - 1))
+        u = (mode - lx // 4).astype(jnp.float32) * (2.0 * np.pi / lx)
+        v = u * u
+        sine = jnp.zeros_like(u)
+        cosine = jnp.zeros_like(u)
+        for n in range(9, -1, -1):
+            sign = -1.0 if n % 2 else 1.0
+            sine = sine * v + sign / float(np.prod(np.arange(1.0, 2 * n + 1)))
+            cosine = cosine * v + sign / float(np.prod(np.arange(1.0, 2 * n + 2)))
+        cosine = -u * cosine
+        kx = (
+            1.5 * sine - 0.6 * sine * cosine + sine * (3.0 - 4.0 * sine * sine) * (1.0 / 30.0)
+        )
+        zero_mode = mode == 0
+        kx = jnp.where(zero_mode, 0.0, kx)
+        ky, kz = plane[2], plane[3]
+        symbol = jnp.zeros_like(kx)
+        for c in range(3):
+            mixed = metric[c, 0] * kx + metric[c, 1] * ky + metric[c, 2] * kz
+            symbol = symbol + mixed * mixed
+        at_edge = zero_mode & (plane[4] > 0.5)
+        total = float(lx * ey * gy * ez * gz)
+        factor[...] = jnp.where(at_edge, 0.0, -1.0 / (jnp.where(at_edge, 1.0, symbol) * total))
+
+    load_plane.wait()
+    make_factor()
+    load_big.wait()
 
     def borders(field, edges, halo, sends, recvs):
         def side(h, edges=edges, halo=halo):
@@ -318,9 +348,6 @@
         + dot(own[0:cells], f1[0]) + dot(own[0:cells], f1[1])
         + dot(own[cells:], f2[0]) + dot(own[cells:], f2[1])
     )
-    load_big.wait()
-    load_plane.wait()
-
     def spread(buffer, h):
         lanes = slice(h * part, (h + 1) * part)
         if rows2 % 8 == 0:
@@ -359,32 +386,6 @@
 
     def share(source, target, send_sem, recv_sem, h):
         return exchange(source, target, send_sem, recv_sem, h, True)
-
-    def make_factor():
-        row = lax.broadcasted_iota(jnp.int32, (2 * m * owners // 2, cells), 0)
-        mode = me * m + (row & (m - 1))
-        u = (mode - lx // 4).astype(jnp.float32) * (2.0 * np.pi / lx)
-        v = u * u
-        sine = jnp.zeros_like(u)
-        cosine = jnp.zeros_like(u)
-        for n in range(9, -1, -1):
-            sign = -1.0 if n % 2 else 1.0
-            sine = sine * v + sign / float(np.prod(np.arange(1.0, 2 * n + 1)))
-            cosine = cosine * v + sign / float(np.prod(np.arange(1.0, 2 * n + 2)))
-        cosine = -u * cosine
-        kx = (
-            1.5 * sine - 0.6 * sine * cosine + sine * (3.0 - 4.0 * sine * sine) * (1.0 / 30.0)
-        )
-        zero_mode = mode == 0
-        kx = jnp.where(zero_mode, 0.0, kx)
-        ky, kz = plane[2], plane[3]
-        symbol = jnp.zeros_like(kx)
-        for c in range(3):
-            mixed = metric[c, 0] * kx + metric[c, 1] * ky + metric[c, 2] * kz
-            symbol = symbol + mixed * mixed
-        at_edge = zero_mode & (plane[4] > 0.5)
-        total = float(lx * ey * gy * ez * gz)
-        factor[...] = jnp.where(at_edge, 0.0, -1.0 / (jnp.where(at_edge, 1.0, symbol) * total))
 
     pending = []
     for h in range(parts):
@@ -406,7 +407,6 @@
         spread(there, h)
         pending.append(exchange(there, here, a_send, a_recv, h))
         pending.append(share(top_line, tops, u_send, u_recv, h))
-    make_factor()
 
     half = lx // 2
     halved = []
@@ -580,7 +580,7 @@
             pl.BlockSpec((block, lx), lambda i: (i + steps, 0)), row,
         ],
         out_specs=(pl.BlockSpec((3, block, lx), lambda i: (0, i, 0)), row),
-        compiler_params=pltpu.CompilerParams(vmem_limit_bytes=32 * 2**20),
+        compiler_params=pltpu.CompilerParams(vmem_limit_bytes=60 * 2**20),
         name="project",
     )(metric, prov, push_x, push_yz, push_yz, heat)
     return motion.reshape(3, ez, ey, lx), heat_next.reshape(ez, ey, lx)

time: 75.9 us -> 72.7 us (0.958)
  local copies, waits for them, and re-layouts: 4.71 us -> 0 us
  Pallas kernels: 70.2 us -> 71.8 us
    unnamed x10 -> x0, local copies, waits for them, and re-layouts: 4.71 us -> none
    pallas_call x1, Pallas kernels: 2.65 us -> 4.25 us  [shards(): pl.pallas_call(project, grid=(steps,), out_shape=(jax.ShapeDtypeStruct((3...]
where the time goes in v7:
time: 72.7 us; the launch traced here: 72.4 us
  Pallas kernels  71.8 us (99%)
    pallas_call x1, Pallas kernels, shards(): pl.pallas_call(lambda *refs: kernel((gy, gz, ez, ey, lx), *refs), out_sha...  67.6 us
    pallas_call x1, Pallas kernels, shards(): pl.pallas_call(project, grid=(steps,), out_shape=(jax.ShapeDtypeStruct((3...  4.25 us

profile of v7, /device:TPU:0, one launch (start us, length us, event | category | flops | bytes accessed | tf_op | source)
XLA Modules:
  0.0 72.4 jit_solution(148656990625865169)
XLA Ops:
  0.6 67.6 %substep.1 = (f32[3,256,512]{2,1,0:T(8,128)}, f32[256,512]{1,0:T(8,128)}, f32[256,512]{1,0:T(8,128)}, f32[512,512]{1,0:T(8,128)}) custom-call(f32[3,3]{1,0:T(4,128)} %metric.1, f32[3,3]{1,0:T(4,128)} %refs_1_.1, bf16[4,256,512]{2,1,0:T(8,128)(2,1)} %bitcast.4, bf16[512,256]{1,0:T(8,128)(2,1)} %constant.14.clone.refs_3_, ...), custom_call_target="tpu_custom_call" | custom-call | flops 4000000000 | bytes 12582912 | tf_op jit(solution)/shard_map/substep/pallas_call | solution.py:520
  68.2 4.2 %project.1 = (f32[3,256,512]{2,1,0:T(8,128)}, f32[256,512]{1,0:T(8,128)}) custom-call(f32[3,3]{1,0:T(4,128)} %metric.1, f32[3,256,512]{2,1,0:T(8,128)} %get-tuple-element.8.prov, f32[256,512]{1,0:T(8,128)} %get-tuple-element.9.push_x, f32[512,512]{1,0:T(8,128)} %get-tuple-element.10.push_y.push_z, f32[512,512]{1,0:T(8,128)} %get-tuple-element.10.push_y.push_z, ...), custom_call_target="tpu_custom_call" | custom-call | tf_op jit(solution)/shard_map/project/pallas_call | solution.py:572

commit v8 on v7

--- a/solution.py
+++ b/solution.py
@@ -133,9 +133,9 @@
 
 
 def kernel(
-    sizes, metric, deform, state, own, beside, beside_sum, pick, along_x, big_hbm, plane_hbm,
-    prov_out, heat_out, push_x_out, push_yz_out,
-    heat_next, big, plane, edge_state, halo_state, grad, grad_x, prov, flux, edge_f, halo_f, div, code_f, code_halo_f, top_f, top_halo_f, tops, top_line,
+    sizes, metric, deform, state_hbm, own_hbm, beside_hbm, beside_sum_hbm, pick, along_x_hbm,
+    big_hbm, plane_hbm, motion_out, heat_out,
+    state, own, beside, beside_sum, along_x, heat_next, big, plane, edge_state, halo_state, grad, grad_x, prov, flux, edge_f, halo_f, div, code_f, code_halo_f, top_f, top_halo_f, tops, top_line,
     edge_p, halo_p, press, line, there, here, there2, here2, factor,
     load_sem, out_sem, t_send, t_recv, u_send, u_recv, s_send, s_recv, f_send, f_recv, p_send, p_recv, a_send, a_recv, b_send, b_recv,
 ):
@@ -155,11 +155,16 @@
     up_z = (iy, lax.rem(iz + 1, gz))
     down_z = (iy, lax.rem(iz + gz - 1, gz))
 
+    load_state = pltpu.make_async_copy(state_hbm, state, load_sem.at[2])
+    load_state.start()
+    loads = [
+        pltpu.make_async_copy(source, target, load_sem.at[3 + k])
+        for k, (source, target) in enumerate(
+            ((own_hbm, own), (along_x_hbm, along_x), (beside_hbm, beside), (beside_sum_hbm, beside_sum))
+        )
+    ]
     load_big = pltpu.make_async_copy(big_hbm, big, load_sem.at[0])
     load_plane = pltpu.make_async_copy(plane_hbm, plane, load_sem.at[1])
-    load_big.start()
-    load_plane.start()
-
     def to_all(begin):
         for dz in range(1, gz):
             begin(iy, lax.rem(iz + dz, gz))
@@ -178,6 +183,11 @@
         pl.semaphore_signal(barrier, inc=1, device_id=(oy, oz), device_id_type=mesh_ids)
 
     to_all(greet)
+    for copy in loads:
+        copy.start()
+    load_plane.start()
+    load_big.start()
+    load_state.wait()
 
     for h in range(parts):
         for c in range(4):
@@ -214,6 +224,8 @@
             s_send.at[2 * parts + 1], s_recv.at[2 * parts + 1], down_z,
         ),
     ]
+    for copy in loads:
+        copy.wait()
     for c in range(4):
         grad[c] = dot(own[...], state[c])
         grad_x[c] = dot(state[c], along_x[...])
@@ -334,8 +346,7 @@
             f_low = low_f()
     f_top = high_f()
     outgoing = [
-        pltpu.make_async_copy(prov, prov_out, out_sem.at[0]),
-        pltpu.make_async_copy(heat_next, heat_out, out_sem.at[1]),
+        pltpu.make_async_copy(heat_next, heat_out, out_sem.at[0]),
     ]
     for copy in outgoing:
         copy.start()
@@ -447,9 +458,19 @@
     p = split(press[...], 3)
     grad[0] = dot(own[...], p[0]) + dot(own[...], p[1]) + dot(own[...], p[2])
     grad_x[0] = dot(p[0], along_x[...]) + dot(p[1], along_x[...]) + dot(p[2], along_x[...])
-    copy = pltpu.make_async_copy(grad_x.at[0], push_x_out, out_sem.at[2])
-    copy.start()
-    outgoing.append(copy)
+
+    def project(i, carry):
+        rows = pl.ds(pl.multiple_of(i * 8, 8), 8)
+        rows_z = pl.ds(pl.multiple_of(cells + i * 8, 8), 8)
+        push = [
+            grad_x[0, rows, :] * sixtieth, grad[0, rows, :] * sixtieth, grad[0, rows_z, :] * sixtieth
+        ]
+        for c in range(3):
+            flux[c, rows, :] = prov[c, rows, :] - (
+                metric[c, 0] * push[0] + metric[c, 1] * push[1] + metric[c, 2] * push[2]
+            )
+        return carry
+
     for h in range(parts):
         for copy in p_side[h]:
             copy.wait()
@@ -462,24 +483,19 @@
         more = dot(beside[h], e[0]) + dot(beside[h], e[1]) + dot(beside[h], e[2])
         grad[0, lo:hi] += more[:part]
         grad[0, cells + lo : cells + hi] += more[part:]
-        for k, rows in enumerate((slice(lo, hi), slice(cells + lo, cells + hi))):
-            copy = pltpu.make_async_copy(
-                grad.at[0, rows], push_yz_out.at[rows], out_sem.at[3 + 2 * h + k]
-            )
-            copy.start()
-            outgoing.append(copy)
+        lax.fori_loop(lo // 8, hi // 8, project, 0)
+        copy = pltpu.make_async_copy(
+            flux.at[:, lo:hi], motion_out.at[:, lo:hi], out_sem.at[1 + h]
+        )
+        copy.start()
+        outgoing.append(copy)
 
     for copy in outgoing:
         copy.wait()
 
 
-def project(metric, prov, push_x, push_y, push_z, heat, motion, heat_next):
-    sixtieth = 1.0 / 60.0
-    push = [push_x[...] * sixtieth, push_y[...] * sixtieth, push_z[...] * sixtieth]
-    for c in range(3):
-        motion[c] = prov[c] - (
-            metric[c, 0] * push[0] + metric[c, 1] * push[1] + metric[c, 2] * push[2]
-        )
+def hand_over(motion, heat, motion_next, heat_next):
+    motion_next[...] = motion[...]
     heat_next[...] = heat[...]
 
 
@@ -517,15 +533,19 @@
     wide = 6 * zc + 4 * ey
     part = zc * ey
     dma = pltpu.SemaphoreType.DMA
-    prov, heat, push_x, push_yz = pl.pallas_call(
+    motion, heat = pl.pallas_call(
         lambda *refs: kernel((gy, gz, ez, ey, lx), *refs),
         out_shape=(
             jax.ShapeDtypeStruct((3, cells, lx), f32), jax.ShapeDtypeStruct((cells, lx), f32),
-            jax.ShapeDtypeStruct((cells, lx), f32), jax.ShapeDtypeStruct((2 * cells, lx), f32),
         ),
-        in_specs=[smem, smem] + [vmem] * 6 + [hbm] * 2,
-        out_specs=(hbm,) * 4,
+        in_specs=[smem, smem] + [hbm] * 4 + [vmem] + [hbm] * 3,
+        out_specs=(hbm,) * 2,
         scratch_shapes=[
+            pltpu.VMEM((4, cells, lx), bf),
+            pltpu.VMEM(own.shape, bf),
+            pltpu.VMEM(beside.shape, bf),
+            pltpu.VMEM((parts, part, wide), bf),
+            pltpu.VMEM((lx, lx), bf),
             pltpu.VMEM((cells, lx), f32),
             pltpu.VMEM(big.shape, bf),
             pltpu.VMEM(plane.shape, f32),
@@ -552,7 +572,7 @@
         + [pltpu.VMEM((parts, owners, 2 * m, part), bf)] * 2
         + [pltpu.VMEM((parts, owners, 2 * m, part), f32)] * 2
         + [pltpu.VMEM((lx // 2, cells), f32)]
-        + [dma((2,)), dma((3 + 2 * parts,))] + [dma((2 * parts,))] * 2 + [dma((parts,))] * 2 + [dma((2 * parts + 2,))] * 6 + [dma((parts,))] * 4,
+        + [dma((7,)), dma((1 + parts,))] + [dma((2 * parts,))] * 2 + [dma((parts,))] * 2 + [dma((2 * parts + 2,))] * 6 + [dma((parts,))] * 4,
         compiler_params=pltpu.CompilerParams(
             collective_id=0, has_side_effects=True, vmem_limit_bytes=56 * 2**20
         ),
@@ -568,21 +588,20 @@
     )
     steps = 4
     block = cells // steps
-    row = pl.BlockSpec((block, lx), lambda i: (i, 0))
+    specs = (
+        pl.BlockSpec((3, block, lx), lambda i: (0, i, 0)), pl.BlockSpec((block, lx), lambda i: (i, 0))
+    )
     motion, heat_next = pl.pallas_call(
-        project,
+        hand_over,
         grid=(steps,),
         out_shape=(
             jax.ShapeDtypeStruct((3, cells, lx), f32), jax.ShapeDtypeStruct((cells, lx), f32)
         ),
-        in_specs=[
-            smem, pl.BlockSpec((3, block, lx), lambda i: (0, i, 0)), row, row,
-            pl.BlockSpec((block, lx), lambda i: (i + steps, 0)), row,
-        ],
-        out_specs=(pl.BlockSpec((3, block, lx), lambda i: (0, i, 0)), row),
+        in_specs=list(specs),
+        out_specs=specs,
         compiler_params=pltpu.CompilerParams(vmem_limit_bytes=60 * 2**20),
-        name="project",
-    )(metric, prov, push_x, push_yz, push_yz, heat)
+        name="hand_over",
+    )(motion, heat)
     return motion.reshape(3, ez, ey, lx), heat_next.reshape(ez, ey, lx)
 
 def solution(mesh):

time: 72.7 us -> 71.8 us (0.988)
  Pallas kernels: 71.8 us -> 71 us
where the time goes in v8:
time: 71.8 us; the launch traced here: 71.6 us
  Pallas kernels  71 us (99%)
    pallas_call x1, Pallas kernels, shards(): pl.pallas_call(lambda *refs: kernel((gy, gz, ez, ey, lx), *refs), out_sha...  67.2 us
    pallas_call x1, Pallas kernels, shards(): pl.pallas_call(hand_over, grid=(steps,), out_shape=(jax.ShapeDtypeStruct(...  3.74 us

profile of v8, /device:TPU:0, one launch (start us, length us, event | category | flops | bytes accessed | tf_op | source)
XLA Modules:
  0.0 71.6 jit_solution(1341686105956367418)
XLA Ops:
  0.6 67.2 %substep.1 = (f32[3,256,512]{2,1,0:T(8,128)}, f32[256,512]{1,0:T(8,128)}) custom-call(f32[3,3]{1,0:T(4,128)} %refs_0_.1, f32[3,3]{1,0:T(4,128)} %refs_1_.1, bf16[4,256,512]{2,1,0:T(8,128)(2,1)} %bitcast.4, bf16[512,256]{1,0:T(8,128)(2,1)} %constant.14.clone.refs_3_, bf16[2,256,128]{2,1,0:T(8,128)(2,1)} %constant.15.clone.refs_4_, ...), custom_call_target="tpu_custom_call" | custom-call | flops 4000000000 | bytes 12582912 | tf_op jit(solution)/shard_map/substep/pallas_call | solution.py:536
  67.9 3.7 %hand_over.1 = (f32[3,256,512]{2,1,0:T(8,128)}, f32[256,512]{1,0:T(8,128)}) custom-call(f32[3,256,512]{2,1,0:T(8,128)} %get-tuple-element.6.motion, f32[256,512]{1,0:T(8,128)} %get-tuple-element.7.heat), custom_call_target="tpu_custom_call" | custom-call | tf_op jit(solution)/shard_map/hand_over/pallas_call | solution.py:594
